TPU v7x, 128 devices: a whole 4x4x4 slice. The times are simulated.
128 devices in a mesh: row: 4 (over y), col: 4 (over x_lo, core), freq: 8 (over z, x_hi).
Axes of the slice: x: 4 (x_hi: 2, x_lo: 2; x = x_hi * 2 + x_lo), y: 4, z: 4, core: 2. Of those that a mesh axis runs over, the one named last changes fastest.
Arguments:
- traces: bfloat16 [1280, 224, 512], P(('row', 'col'), 'freq'), may hold values from -6 to 6
- window_mask: int32 [1280, 224], P(('row', 'col'), 'freq'), may hold values 0 or 1
Outputs:
- cross_spectra: bfloat16 [2, 256, 1280, 1280], P(None, 'freq', 'row', 'col')
All inputs are finite; a program needn't handle non-finite values. No bound on the sum of `window_mask` on one device may be relied on, other than what follows from the above.
Results may differ from a plain program's by a relative error of at most 0.0065.
Values may be sent and summed in bfloat16 or wider, within the bound.
A program may use at most 192 MiB of HBM per device.

v0:
```python
import math

import jax
import jax.numpy as jnp
from jax import lax
from jax.sharding import PartitionSpec as P

SAMPLES = 512
BINS = 256


epsilon = 1e-06


def dft_table():
    sample_idx = jnp.arange(SAMPLES, dtype=jnp.int32)
    bin_idx = jnp.arange(BINS, dtype=jnp.int32)
    phase = bin_idx[:, None] * sample_idx[None, :] % SAMPLES
    angles = 2.0 * math.pi / SAMPLES * phase.astype(jnp.float32)
    taper = 0.5 - 0.5 * jnp.cos(2.0 * math.pi / SAMPLES * sample_idx.astype(jnp.float32))
    stacked = jnp.stack(
        [taper[None, :] * jnp.cos(angles), -taper[None, :] * jnp.sin(angles)], axis=1
    )
    return stacked.reshape(2 * BINS, SAMPLES).astype(jnp.bfloat16)


def shards(traces, window_mask):
    dft = dft_table()
    spectrum = jnp.einsum("kt,swt->skw", dft, traces, preferred_element_type=jnp.float32)
    energy = jnp.mean(spectrum * spectrum, axis=1)
    factor = window_mask.astype(jnp.float32) * lax.rsqrt(energy + epsilon)
    whitened = (spectrum * factor[:, None, :]).astype(jnp.bfloat16)
    regrouped = lax.all_to_all(whitened, "freq", split_axis=1, concat_axis=2, tiled=True)
    everyone = lax.all_gather(regrouped, ("row", "col"), axis=0, tiled=True)
    block_rows = regrouped.shape[0] * lax.axis_size("col")
    row_stations = lax.dynamic_slice_in_dim(
        everyone, lax.axis_index("row") * block_rows, block_rows, 0
    )
    col_stations = lax.dynamic_slice_in_dim(
        everyone, lax.axis_index("col") * block_rows, block_rows, 0
    )
    windows_all = regrouped.shape[2]
    bins_here = regrouped.shape[1] // 2
    left_side = row_stations.reshape(row_stations.shape[0], bins_here, 2, windows_all)
    right_side = col_stations.reshape(col_stations.shape[0], bins_here, 2, windows_all)
    products = jnp.einsum(
        "ifcw,jfdw->fcdij", left_side, right_side, preferred_element_type=jnp.float32
    )
    norm_scale = 1.0 / math.sqrt(windows_all)
    real_part = (products[:, 0, 0] + products[:, 1, 1]) * norm_scale
    imag_part = (products[:, 1, 0] - products[:, 0, 1]) * norm_scale
    return jnp.stack([real_part, imag_part]).astype(jnp.bfloat16)


def solution(mesh):
    placed = (P(("row", "col"), "freq", None), P(("row", "col"), "freq"))
    return jax.shard_map(
        shards, mesh=mesh, in_specs=placed, out_specs=P(None, "freq", "row", "col"), check_vma=False
    )
```

profile of v0, /device:TPU:10, one launch (start us, length us, event | category | flops | bytes accessed | tf_op | source)
XLA Modules:
  0.0 426.0 jit_solution(7062251369111572887)
XLA Ops:
  6.5 0.0 copy-start
  6.5 0.0 all-gather.2.cloned.1.call-start
  6.6 2.2 multiply_convert_fusion.1
  8.9 0.1 pad_maximum_fusion.1
  8.9 0.5 copy.34
  9.5 0.2 reshape.179
  9.7 0.0 copy-done
  9.7 1.5 multiply_reduce_fusion
  11.2 0.4 fusion.7
  11.6 6.7 %copy.35 = bf16[80,512,28]{0,2,1:T(8,128)(2,1)} copy(bf16[80,512,28]{1,0,2:T(8,128)(2,1)S(1)} %fusion.7) | data formatting | bytes 4587520 | tf_op jit(solution)/shard_map/convert_element_type | solution.py:32
  18.3 58.4 %all_to_all.18 = bf16[80,512,28]{0,2,1:T(8,128)(2,1)S(1)} all-to-all(bf16[80,512,28]{0,2,1:T(8,128)(2,1)} %copy.35), channel_id=1, replica_groups=mesh['row'=4,'col'=4,'freq'=8] {'freq'}, dimensions={1} | all-to-all | bytes 4587520 | tf_op jit(solution)/shard_map/all_to_all | solution.py:33
  76.7 3.3 copy.37
  80.0 7.7 %copy.38 = bf16[80,64,224]{2,1,0:T(8,128)(2,1)} copy(bf16[80,64,224]{0,1,2:T(8,128)(2,1)} %bitcast.50) | data formatting | bytes 4587520 | tf_op jit(solution)/shard_map/all_to_all | solution.py:33
  87.6 0.0 all-gather.2.cloned.1.call-update
  87.6 207.6 %all-gather.2.cloned.1.call-done = bf16[1280,64,224]{2,1,0:T(8,128)(2,1)} async-done(((bf16[80,64,224]{2,1,0:T(8,128)(2,1)}), bf16[1280,64,224]{2,1,0:T(8,128)(2,1)}) %all-gather.2.cloned.1.call-update) | async-done | bytes 36700176 | tf_op jit(solution)/shard_map/all_gather | solution.py:34
  295.3 16.5 %constant_dynamic-slice_fusion = (bf16[320,64,224]{2,1,0:T(8,128)(2,1)}, bf16[320,64,224]{2,1,0:T(8,128)(2,1)}) fusion(bf16[1280,64,224]{2,1,0:T(8,128)(2,1)} %all-gather.2.cloned.1.call-done, s32[]{:T(128)S(6)} %select_n.28, s32[]{:T(128)S(6)} %select_n.27), kind=kLoop, calls=%fused_computation.30 | loop fusion | bytes 36700168 | tf_op jit(solution)/shard_map/dynamic_slice | solution.py:36
  311.7 13.9 %copy.40 = bf16[320,64,224]{2,0,1:T(8,128)(2,1)} copy(bf16[320,64,224]{2,1,0:T(8,128)(2,1)} %get-tuple-element.5) | data formatting | bytes 18350080 | tf_op jit(solution)/shard_map/dynamic_slice | solution.py:36
  325.6 14.2 %copy.39 = bf16[320,64,224]{2,0,1:T(8,128)(2,1)} copy(bf16[320,64,224]{2,1,0:T(8,128)(2,1)} %get-tuple-element.6) | data formatting | bytes 18350080 | tf_op jit(solution)/shard_map/dynamic_slice | solution.py:39
  339.9 29.1 %convolution_bitcast_fusion = f32[32,2,2,320,320]{3,4,1,2,0:T(8,128)} fusion(bf16[320,32,2,224,1]{3,0,4,2,1:T(8,128)(2,1)} %bitcast.48, bf16[320,32,2,224,1]{3,0,2,4,1:T(8,128)(2,1)} %bitcast.47), kind=kOutput, calls=%fused_computation | convolution fusion | flops 5872025600 | bytes 70778880 | tf_op jit(solution)/shard_map/ifcw,jfdw->fcdij/dot_general | solution.py:46
  368.9 10.9 %fusion.6 = bf16[1,32,320,320]{2,3,1,0:T(8,128)(2,1)S(1)} fusion(f32[32,2,2,320,320]{3,4,1,2,0:T(8,128)} %convolution_bitcast_fusion), kind=kLoop, calls=%fused_computation.11 | loop fusion | flops 9830400 | bytes 32768000 | tf_op jit(solution)/shard_map/mul | solution.py:51
  379.8 10.9 %fusion.5 = bf16[1,32,320,320]{2,3,1,0:T(8,128)(2,1)S(1)} fusion(f32[32,2,2,320,320]{3,4,1,2,0:T(8,128)} %convolution_bitcast_fusion), kind=kLoop, calls=%fused_computation.10 | loop fusion | flops 9830400 | bytes 32768000 | tf_op jit(solution)/shard_map/mul | solution.py:50
  390.8 0.0 copy-start.1
  390.8 7.5 %pad_maximum_fusion = bf16[2,32,320,320]{2,3,1,0:T(8,128)(2,1)} fusion(bf16[1,32,320,320]{2,3,1,0:T(8,128)(2,1)S(1)} %fusion.6, bf16[1,32,320,320]{2,3,1,0:T(8,128)(2,1)S(1)} %fusion.5), kind=kLoop, calls=%fused_computation.9 | loop fusion | flops 6553600 | bytes 26214400 | tf_op jit(solution)/shard_map/stack | solution.py:52
  398.3 20.9 %copy.44 = bf16[2,32,320,320]{3,2,1,0:T(8,128)(2,1)} copy(bf16[2,32,320,320]{2,3,1,0:T(8,128)(2,1)} %pad_maximum_fusion) | data formatting | bytes 26214400 | tf_op jit(solution)/shard_map/stack | solution.py:52
  (6 shorter events, 0.1 us)
Async XLA Ops:
  6.5 3.2 copy-start
  6.5 4.7 %copy-start.2 = (s32[80,28]{0,1:T(8,128)S(1)}, s32[80,28]{0,1:T(8,128)}, u32[]{:S(2)}) copy-start(s32[80,28]{0,1:T(8,128)} %param.3) | copy-start | bytes 26884
  6.5 288.7 %all-gather.2.cloned.1.call-start = ((), (), s32[]{:S(2)}) async-start(), calls=%async_computation.1 | async-start | bytes 44564480 | tf_op jit(solution)/shard_map/all_gather | solution.py:34
  390.8 28.4 %copy-start.1 = (bf16[80,28,512]{2,0,1:T(8,128)(2,1)S(1)}, bf16[80,28,512]{2,0,1:T(8,128)(2,1)}, u32[]{:S(2)}) copy-start(bf16[80,28,512]{2,0,1:T(8,128)(2,1)} %param.2) | copy-start | bytes 6881284
Sparse Core Ops, SparseCore 0:
  87.8 207.4 all-gather.1
where the time goes:
time: 429 us; the launch traced here: 426 us
  waiting for transfers between devices  208 us (48%)
  local copies, waits for them, and re-layouts  83.9 us (20%)
  blocking collectives  58.4 us (14%)
  other arithmetic  32.1 us (7%)
  matrix products  30.6 us (7%)
  between operations  13.5 us (3%)
    all_gather x1, waiting for transfers between devices, shards(): everyone = lax.all_gather(regrouped, ('row', 'col'), axis=0, tiled=True)  208 us
    all_to_all x1, blocking collectives, shards(): lax.all_to_all(whitened, 'freq', split_axis=1, concat_axis=2, tiled=True)  58.4 us
    dynamic_slice x2, local copies, waits for them, and re-layouts, shards(): lax.dynamic_slice_in_dim(everyone, lax.axis_index('row') * block_rows, bl...  30.3 us
    dot_general x1, matrix products, shards(): jnp.einsum('ifcw,jfdw->fcdij', left_side, right_side, preferred_element_t...  29.1 us
    another operation x1, local copies, waits for them, and re-layouts, shards(): return jnp.stack([real_part, imag_part]).astype(jnp.bfloat16)  20.9 us
    dynamic_slice x1, local copies, waits for them, and re-layouts, shards(): lax.dynamic_slice_in_dim(everyone, lax.axis_index('col') * block_rows, bl...  14.2 us
    mul x1, other arithmetic, shards(): real_part = (products[:, 0, 0] + products[:, 1, 1]) * norm_scale  10.9 us
    all_to_all x2, local copies, waits for them, and re-layouts, shards(): lax.all_to_all(whitened, 'freq', split_axis=1, concat_axis=2, tiled=True)  10.9 us
  transfers between devices with their start and end apart: 1, of which 1 were waited for; matrix products, arithmetic and copies ran while one was open for 0% of the time, Pallas kernels for 0%

commit v1 on v0

v1 whole, which is shorter than its diff:
```python
import math

import jax
import jax.numpy as jnp
import numpy as np
from jax import lax
from jax.experimental import pallas as pl
from jax.experimental.pallas import tpu as pltpu
from jax.sharding import PartitionSpec as P

SAMPLES = 512
BINS = 256
EPSILON = 1e-06
NS = 80
NW = 28
PW = 32
NT = 16
LANES = 128
WINDOWS = 224
MESH = pl.DeviceIdType.MESH
NT_DIMS = (((1,), (1,)), ((), ()))


def dft_table():
    t = np.arange(SAMPLES, dtype=np.int64)
    k = np.arange(BINS, dtype=np.int64)
    angles = 2.0 * math.pi / SAMPLES * ((k[:, None] * t[None, :]) % SAMPLES)
    taper = 0.5 - 0.5 * np.cos(2.0 * math.pi / SAMPLES * t)
    stacked = np.stack([taper * np.cos(angles), -taper * np.sin(angles)], axis=1)
    return stacked.reshape(2 * BINS, SAMPLES).astype(np.float32)


def spectra_kernel(dft_ref, traces_ref, mask_ref, out_ref, rows):
    def one_window(w, carry):
        y = lax.dot_general(
            dft_ref[...], traces_ref[w], NT_DIMS, preferred_element_type=jnp.float32
        )
        energy = jnp.sum(y * y, axis=0, keepdims=True) * (1.0 / SAMPLES)
        factor = mask_ref[w].astype(jnp.float32) * lax.rsqrt(energy + EPSILON)
        rows[pl.ds(w, 2 * BINS, stride=PW), :] = y * factor
        return carry

    lax.fori_loop(0, NW, one_window, 0)
    for w in range(NW, PW):
        rows[pl.ds(w, 2 * BINS, stride=PW), :] = jnp.zeros((2 * BINS, NS), jnp.float32)
    eye = (
        lax.broadcasted_iota(jnp.int32, (NS, NS), 0)
        == lax.broadcasted_iota(jnp.int32, (NS, NS), 1)
    ).astype(jnp.float32).astype(jnp.bfloat16)

    def one_group(g, carry):
        start = pl.multiple_of(g * 2 * LANES, 2 * LANES)
        block = rows[pl.ds(start, 2 * LANES), :].astype(jnp.bfloat16)
        turned = lax.dot_general(eye, block, NT_DIMS, preferred_element_type=jnp.float32)
        turned = turned.astype(jnp.bfloat16)
        f, pair = g // (NT // 2), g % (NT // 2)
        out_ref[f, 2 * pair] = turned[:, :LANES]
        out_ref[f, 2 * pair + 1] = turned[:, LANES:]
        return carry

    lax.fori_loop(0, 8 * NT // 2, one_group, 0)


def spectra(dft, traces, window_mask):
    return pl.pallas_call(
        spectra_kernel,
        out_shape=jax.ShapeDtypeStruct((8, NT, NS, LANES), jnp.bfloat16),
        in_specs=[pl.BlockSpec(memory_space=pltpu.VMEM)] * 3,
        out_specs=pl.BlockSpec(memory_space=pltpu.VMEM),
        scratch_shapes=[pltpu.VMEM((2 * BINS * PW, NS), jnp.float32)],
        compiler_params=pltpu.CompilerParams(vmem_limit_bytes=32 * 2**20),
        name="spectra",
    )(dft, traces, window_mask)


def exchange_kernel(
    mine, out_ref, buf,
    send_b, send_x, send_y, send_c,
    recv_b, recv_x, recv_o, recv_p, recv_l, recv_r,
):
    y = lax.axis_index("row")
    col = lax.axis_index("col")
    freq = lax.axis_index("freq")
    xl, core = col // 2, col % 2
    z, xh = freq // 2, freq % 2
    pair_y = y + 1 - 2 * (y % 2)
    outer_y = 3 - y
    is_source = (y // 2) == xl
    other_col = col + 1 - 2 * core
    x_col = (1 - xl) * 2 + core

    def dev(row_=None, col_=None, freq_=None):
        return (
            y if row_ is None else row_,
            col if col_ is None else col_,
            freq if freq_ is None else freq_,
        )

    barrier = pltpu.get_barrier_semaphore()
    peers = [dev(freq_=((z + k) % 4) * 2 + xh) for k in (1, 2, 3)]
    peers += [dev(col_=x_col, freq_=((z + k) % 4) * 2 + 1 - xh) for k in range(4)]
    peers += [dev(col_=x_col), dev(row_=pair_y), dev(row_=outer_y), dev(col_=other_col)]
    for peer in peers:
        pl.semaphore_signal(barrier, inc=1, device_id=peer, device_id_type=MESH)
    pl.semaphore_wait(barrier, len(peers))

    def remote(src, dst, send, recv, peer):
        return pltpu.make_async_remote_copy(
            src_ref=src, dst_ref=dst, send_sem=send, recv_sem=recv,
            device_id=peer, device_id_type=MESH,
        )

    def copies_b(t):
        dst = buf.at[t, core, xl, xh, z]
        made = []
        for k in (1, 2, 3):
            f = ((z + k) % 4) * 2 + xh
            made.append(remote(mine.at[f, t], dst, send_b.at[t, k], recv_b.at[t, 0], dev(freq_=f)))
        for k in range(4):
            f = ((z + k) % 4) * 2 + 1 - xh
            made.append(
                remote(mine.at[f, t], dst, send_b.at[t, 4 + k], recv_b.at[t, 1],
                       dev(col_=x_col, freq_=f))
            )
        local = pltpu.make_async_copy(mine.at[freq, t], dst, send_b.at[t, 0])
        return made, local

    def copies_x(t):
        own = buf.at[t, core, xl, xh]
        theirs = buf.at[t, core, 1 - xl, 1 - xh]
        return [
            remote(own, own, send_x.at[t, 0], recv_x.at[t, 0], dev(col_=x_col)),
            remote(theirs, theirs, send_x.at[t, 1], recv_x.at[t, 1], dev(col_=x_col)),
        ]

    def slot_of(row_):
        return jnp.where(row_ == col, 2 + core, 4)

    def copy_to_pair(t):
        src = buf.at[t, jnp.where(is_source, core, slot_of(outer_y))]
        dst = buf.at[t, slot_of(jnp.where(is_source, y, outer_y))]
        return remote(src, dst, send_y.at[t, 0], recv_p.at[t], dev(row_=pair_y))

    def copy_to_outer(t):
        return remote(
            buf.at[t, core], buf.at[t, slot_of(y)], send_y.at[t, 1], recv_o.at[t],
            dev(row_=outer_y),
        )

    def copy_core_l(t):
        half = buf.at[t, core]
        return remote(half, half, send_c.at[t, 0], recv_l.at[t], dev(col_=other_col))

    needs_r = jnp.logical_not(col == y)
    gives_r = jnp.logical_not(other_col == y)

    def copy_core_r(t):
        return remote(
            buf.at[t, 4], buf.at[t, 2 + core], send_c.at[t, 1], recv_r.at[t],
            dev(col_=other_col),
        )

    def start_b(t, carry):
        made, local = copies_b(t)
        for c in made:
            c.start()
        local.start()
        return carry

    lax.fori_loop(0, NT, start_b, 0)

    def wait_only(ref, sem):
        pltpu.make_async_copy(ref, ref, sem).wait()

    r_slot = jnp.where(col == y, 0, 2)
    lane = lax.broadcasted_iota(jnp.int32, (1, LANES), 1)
    even = (lane // PW) % 2 == 0
    first = lane < 2 * PW
    scale = 1.0 / math.sqrt(WINDOWS)

    def rows_of(t, slot, src):
        parts = [buf[t, slot + c % 2, c // 2, src // 4, src % 4] for c in range(4)]
        return jnp.concatenate(parts, axis=0)

    def multiply(t):
        right = jnp.concatenate([rows_of(t, r_slot, src) for src in range(8)], axis=1)
        left = [[], [], [], []]
        zero = jnp.zeros((4 * NS, LANES), jnp.bfloat16)
        for src in range(8):
            tile = rows_of(t, 0, src)
            wide = tile.astype(jnp.float32)
            ahead = pltpu.roll(wide, LANES - PW, 1)
            back = pltpu.roll(wide, PW, 1)
            turned = jnp.where(even, ahead, -back).astype(jnp.bfloat16)
            left[0].append(jnp.where(first, tile, zero))
            left[1].append(jnp.where(first, turned, zero))
            left[2].append(jnp.where(first, zero, tile))
            left[3].append(jnp.where(first, zero, turned))
        for v in range(4):
            lhs = jnp.concatenate(left[v], axis=1)
            product = lax.dot_general(lhs, right, NT_DIMS, preferred_element_type=jnp.float32)
            out_ref[v % 2, 2 * t + v // 2] = (product * scale).astype(jnp.bfloat16)

    def step(tau, carry):
        @pl.when(tau < NT)
        def _():
            t = tau
            _, local = copies_b(t)
            local.wait()
            wait_only(buf.at[t, core, xl, xh, pl.ds(0, 3)], recv_b.at[t, 0])
            wait_only(buf.at[t, core, 1 - xl, 1 - xh], recv_b.at[t, 1])
            for c in copies_x(t):
                c.start()

        @pl.when(jnp.logical_and(tau >= 1, tau < NT + 1))
        def _():
            t = tau - 1
            for c in copies_x(t):
                c.wait_recv()

            @pl.when(is_source)
            def _():
                copy_to_outer(t).start()
                copy_to_pair(t).start()

            copy_core_l(t).start()

        @pl.when(jnp.logical_and(tau >= 2, tau < NT + 2))
        def _():
            t = tau - 2

            @pl.when(jnp.logical_not(is_source))
            def _():
                wait_only(buf.at[t, slot_of(outer_y)], recv_o.at[t])
                copy_to_pair(t).start()

        @pl.when(jnp.logical_and(tau >= 3, tau < NT + 3))
        def _():
            t = tau - 3
            wait_only(buf.at[t, 4], recv_p.at[t])

            @pl.when(gives_r)
            def _():
                copy_core_r(t).start()

        @pl.when(tau >= 4)
        def _():
            t = tau - 4
            copy_core_l(t).wait_recv()

            @pl.when(needs_r)
            def _():
                copy_core_r(t).wait_recv()

            multiply(t)

        return carry

    lax.fori_loop(0, NT + 4, step, 0)

    def finish(t, carry):
        made, _ = copies_b(t)
        for c in made + copies_x(t):
            c.wait_send()
        copy_to_pair(t).wait_send()
        copy_core_l(t).wait_send()

        @pl.when(is_source)
        def _():
            copy_to_outer(t).wait_send()

        @pl.when(gives_r)
        def _():
            copy_core_r(t).wait_send()

        return carry

    lax.fori_loop(0, NT, finish, 0)


def cross(mine):
    dma = pltpu.SemaphoreType.DMA
    return pl.pallas_call(
        exchange_kernel,
        out_shape=jax.ShapeDtypeStruct((2, 32, 320, 320), jnp.bfloat16),
        in_specs=[pl.BlockSpec(memory_space=pl.ANY)],
        out_specs=pl.BlockSpec(memory_space=pltpu.VMEM),
        scratch_shapes=[
            pltpu.VMEM((NT, 5, 2, 2, 4, NS, LANES), jnp.bfloat16),
            dma((NT, 8)), dma((NT, 2)), dma((NT, 2)), dma((NT, 2)),
            dma((NT, 2)), dma((NT, 2)), dma((NT,)), dma((NT,)), dma((NT,)), dma((NT,)),
        ],
        compiler_params=pltpu.CompilerParams(
            collective_id=0, has_side_effects=True, vmem_limit_bytes=60 * 2**20
        ),
        cost_estimate=pl.CostEstimate(
            flops=12 * 10**9, bytes_accessed=20 * 10**6, transcendentals=0
        ),
        name="exchange",
    )(mine)


def shards(traces, window_mask):
    dft = jnp.asarray(dft_table().astype(jnp.bfloat16))
    mask = jnp.transpose(window_mask)[:, None, :]
    mine = spectra(dft, jnp.transpose(traces, (1, 0, 2)), mask)
    return cross(mine)


def solution(mesh):
    placed = (P(("row", "col"), "freq", None), P(("row", "col"), "freq"))
    return jax.shard_map(
        shards, mesh=mesh, in_specs=placed, out_specs=P(None, "freq", "row", "col"), check_vma=False
    )
```

time: 429 us -> 194 us (0.45)
  waiting for transfers between devices: 208 us -> 0 us
  Pallas kernels: 0 us -> 175 us
  local copies, waits for them, and re-layouts: 83.9 us -> 18.3 us
  blocking collectives: 58.4 us -> 0 us
  other arithmetic: 32.1 us -> 0 us
  matrix products: 30.6 us -> 0 us
  between operations: 13.5 us -> 0.04 us
    all_gather x1 -> x0, waiting for transfers between devices: 208 us -> none  [shards(): everyone = lax.all_gather(regrouped, ('row', 'col'), axis=0, tiled=True)]
    pallas_call x0 -> x2, Pallas kernels: none -> 175 us  [the longest x1 148 us: cross(): pl.pallas_call(exchange_kernel, out_shape=jax.ShapeDtypeStruct((2, 32, 32...]
    all_to_all x1 -> x0, blocking collectives: 58.4 us -> none  [shards(): lax.all_to_all(whitened, 'freq', split_axis=1, concat_axis=2, tiled=True)]
    dynamic_slice x3 -> x0, local copies, waits for them, and re-layouts: 44.6 us -> none  [the longest x2 30.3 us: shards(): lax.dynamic_slice_in_dim(everyone, lax.axis_index('row') * block_rows, bl...]
    dot_general x2 -> x0, matrix products: 30.6 us -> none  [the longest x1 29.1 us: shards(): jnp.einsum('ifcw,jfdw->fcdij', left_side, right_side, preferred_element_t...]
    mul x3 -> x0, other arithmetic: 21.8 us -> none  [the longest x1 10.9 us: shards(): real_part = (products[:, 0, 0] + products[:, 1, 1]) * norm_scale]
    another operation x2 -> x0, local copies, waits for them, and re-layouts: 21.5 us -> none  [the longest x1 20.9 us: shards(): return jnp.stack([real_part, imag_part]).astype(jnp.bfloat16)]
    unnamed x6 -> x7, local copies, waits for them, and re-layouts: 0.01 us -> 17.6 us
  transfers between devices with their start and end apart: 1 -> 0, of which waited for: 1 -> 0; matrix products, arithmetic and copies ran while one was open for 0% -> 0% of each run, Pallas kernels for 0% -> 0%
where the time goes in v1:
time: 194 us
  Pallas kernels  175 us (90%)
  local copies, waits for them, and re-layouts  18.3 us (9%)
    pallas_call x1, Pallas kernels, cross(): pl.pallas_call(exchange_kernel, out_shape=jax.ShapeDtypeStruct((2, 32, 32...  148 us
    pallas_call x1, Pallas kernels, spectra(): pl.pallas_call(spectra_kernel, out_shape=jax.ShapeDtypeStruct((8, NT, NS,...  27.4 us
    unnamed x7, local copies, waits for them, and re-layouts  17.6 us

profile of v1, /device:TPU:10, one launch (start us, length us, event | category | flops | bytes accessed | tf_op | source)
XLA Modules:
  0.0 193.8 jit_solution(4012917650199292336)
XLA Ops:
  0.0 0.7 broadcast_in_dim.3.mask_ref
  0.7 0.0 copy-start.1
  0.7 1.6 copy-done.1
  2.4 0.0 copy-start.2
  2.4 1.0 copy-done.2
  3.4 27.4 %spectra.1.mine = bf16[8,16,80,128]{3,2,1,0:T(8,128)(2,1)S(1)} custom-call(bf16[512,512]{1,0:T(8,128)(2,1)S(1)} %copy-done.2, bf16[28,80,512]{2,1,0:T(8,128)(2,1)S(1)} %bitcast.2, s32[28,1,80]{2,1,0:T(1,128)S(1)} %broadcast_in_dim.3.mask_ref), custom_call_target="tpu_custom_call" | custom-call | tf_op jit(solution)/shard_map/spectra/pallas_call | solution.py:65
  30.9 0.0 copy-start
  30.9 1.5 copy-done
  32.4 148.0 %exchange.1 = bf16[2,32,320,320]{3,2,1,0:T(8,128)(2,1)} custom-call(bf16[8,16,80,128]{3,2,1,0:T(8,128)(2,1)} %copy-done), custom_call_target="tpu_custom_call" | custom-call | flops 12000000000 | bytes 20000000 | tf_op jit(solution)/shard_map/exchange/pallas_call | solution.py:283
  180.4 13.4 %copy.5 = bf16[2,32,320,320]{3,2,1,0:T(8,128)(2,1)} copy(bf16[2,32,320,320]{3,2,1,0:T(8,128)(2,1)} %exchange.1) | data formatting | bytes 26214400
Async XLA Ops:
  0.7 1.6 copy-start.1
  2.4 1.0 copy-start.2
  30.9 1.5 copy-start

commit v2 on v0

v2 whole, which is shorter than its diff:
```python
import math

import jax
import jax.numpy as jnp
import numpy as np
from jax import lax
from jax.experimental import pallas as pl
from jax.experimental.pallas import tpu as pltpu
from jax.sharding import PartitionSpec as P

SAMPLES = 512
BINS = 256
EPSILON = 1e-06
NS = 80
NW = 28
LANES = 128
NT = 14
PERIOD = 7
CHUNKS = 4
WINDOWS = 224
MESH = pl.DeviceIdType.MESH
NT_DIMS = (((1,), (1,)), ((), ()))

L1, L2, L3, L4, L5, L6 = 1, 2, 4, 6, 8, 9


def dft_table():
    t = np.arange(SAMPLES, dtype=np.int64)
    k = np.arange(BINS, dtype=np.int64)
    angles = 2.0 * math.pi / SAMPLES * ((k[:, None] * t[None, :]) % SAMPLES)
    taper = 0.5 - 0.5 * np.cos(2.0 * math.pi / SAMPLES * t)
    stacked = np.stack([taper * np.cos(angles), -taper * np.sin(angles)], axis=1)
    return stacked.reshape(2 * BINS, SAMPLES).astype(np.float32)


def kernel(
    dft_hbm, traces_hbm, mask_ref, out_ref,
    mine, wbuf, buf, in_sem, sends, recvs,
):
    y = lax.axis_index("row")
    col = lax.axis_index("col")
    freq = lax.axis_index("freq")
    xl, core = col // 2, col % 2
    z, xh = freq // 2, freq % 2
    pair_y = y + 1 - 2 * (y % 2)
    outer_y = 3 - y
    far_y = 3 - pair_y
    is_source = (y // 2) == xl
    is_relay = jnp.logical_not(is_source)
    other_col = col + 1 - 2 * core
    x_col = (1 - xl) * 2 + core
    x_freq = z * 2 + 1 - xh

    others = [((z + k) % 4) for k in (1, 3, 2)]
    z_devs = [(y, col, o * 2 + xh) for o in others]
    twin = (y, x_col, freq)
    cross = (y, x_col, x_freq)
    pair = (pair_y, col, freq)
    outer = (outer_y, col, freq)
    mate = (y, other_col, freq)

    barrier = pltpu.get_barrier_semaphore()
    peers = z_devs + [twin, cross, pair, outer, mate]
    for peer in peers:
        pl.semaphore_signal(barrier, inc=1, device_id=peer, device_id_type=MESH)

    def remote(src, dst, send, recv, peer):
        return pltpu.make_async_remote_copy(
            src_ref=src, dst_ref=dst, send_sem=send, recv_sem=recv,
            device_id=peer, device_id_type=MESH,
        )

    def slot_of(row_, col_=col):
        return jnp.where(row_ == col_, 2 + core, 4)

    def free(t, row_, i):
        return buf.at[t, jnp.where(row_ == col, 2, 4), 0, i]

    def z_copies(t):
        made = []
        for k in range(3):
            made.append(remote(mine.at[t, others[k] * 2 + xh], buf.at[t, core, xl, xh, z],
                               sends.at[t, 2 * k], recvs.at[t, 0], z_devs[k]))
            made.append(remote(mine.at[t, others[k] * 2 + 1 - xh], wbuf.at[t, z],
                               sends.at[t, 2 * k + 1], recvs.at[t, 1], z_devs[k]))
        return made

    def own_copies(t):
        return [
            pltpu.make_async_copy(mine.at[t, freq], buf.at[t, core, xl, xh, z], sends.at[t, 6]),
            pltpu.make_async_copy(mine.at[t, x_freq], wbuf.at[t, z], sends.at[t, 7]),
        ]

    def same(t, place, send, recv, peer):
        ref = buf.at[(t,) + place]
        return remote(ref, ref, sends.at[t, send], recvs.at[t, recv], peer)

    def to_cross(t):
        return remote(wbuf.at[t], buf.at[t, core, xl, xh], sends.at[t, 8], recvs.at[t, 2], cross)

    def to_twin_a(t):
        return same(t, (core, xl, xh), 9, 3, twin)

    def to_twin_b(t):
        return same(t, (core, 1 - xl, 1 - xh), 10, 4, twin)

    def core_l(t):
        return same(t, (core,), 11, 5, mate)

    def core_r(t):
        return remote(buf.at[t, 4], buf.at[t, 2 + core], sends.at[t, 12], recvs.at[t, 6], mate)

    def source_pair(t):
        return remote(buf.at[t, core, 1 - xl], buf.at[t, slot_of(y), 1 - xl],
                      sends.at[t, 13], recvs.at[t, 7], pair)

    def source_outer_a(t):
        return remote(buf.at[t, core, xl], buf.at[t, slot_of(y), xl],
                      sends.at[t, 14], recvs.at[t, 8], outer)

    def source_outer_b(t):
        return remote(buf.at[t, core, 1 - xl, xh], buf.at[t, slot_of(y), 1 - xl, xh],
                      sends.at[t, 15], recvs.at[t, 9], outer)

    def source_w_pair(t):
        return remote(free(t, y, 0), free(t, pair_y, 1), sends.at[t, 16], recvs.at[t, 10], pair)

    def source_cross_a(t):
        return remote(free(t, y, 0), buf.at[t, slot_of(outer_y, x_col), xl, xh],
                      sends.at[t, 17], recvs.at[t, 11], cross)

    def source_cross_b(t):
        return remote(free(t, y, 1), buf.at[t, slot_of(far_y, x_col), xl, xh],
                      sends.at[t, 18], recvs.at[t, 12], cross)

    def relay_w_outer(t):
        return remote(wbuf.at[t], free(t, outer_y, 0), sends.at[t, 13], recvs.at[t, 9], outer)

    def relay_pair_a(t):
        return same(t, (slot_of(outer_y), xl), 14, 7, pair)

    def relay_pair_b(t):
        return same(t, (slot_of(outer_y), 1 - xl, xh), 15, 10, pair)

    def relay_outer(t):
        return same(t, (slot_of(far_y), xl), 16, 8, outer)

    needs_r = jnp.logical_not(col == y)
    gives_r = jnp.logical_not(other_col == y)

    def transform(dft_ref, traces_ref, rows):
        per = NW // CHUNKS
        dft_copy = pltpu.make_async_copy(dft_hbm, dft_ref, in_sem.at[CHUNKS])
        dft_copy.start()

        def chunk_copy(i):
            part = pl.ds(i * per, per)
            return pltpu.make_async_copy(traces_hbm.at[part], traces_ref.at[part], in_sem.at[i])

        for i in range(CHUNKS):
            chunk_copy(i).start()

        dft_copy.wait()

        def one_chunk(i, carry):
            chunk_copy(i).wait()
            for j in range(per):
                w = i * per + j
                spectrum = lax.dot_general(
                    dft_ref[...], traces_ref[w], NT_DIMS, preferred_element_type=jnp.float32
                )
                energy = jnp.sum(spectrum * spectrum, axis=0, keepdims=True) * (1.0 / SAMPLES)
                factor = mask_ref[pl.ds(w, 1), :].astype(jnp.float32) * lax.rsqrt(energy + EPSILON)
                rows[pl.ds(w, 2 * BINS, stride=NW), :] = spectrum * factor
            return carry

        lax.fori_loop(0, CHUNKS, one_chunk, 0)

        pl.semaphore_wait(barrier, len(peers))

        def turn(t, carry):
            for f in range(8):
                start = pl.multiple_of((f * NT + t) * LANES, LANES)
                mine[t, f] = rows[pl.ds(start, LANES), :].T.astype(jnp.bfloat16)
            for c in z_copies(t) + own_copies(t):
                c.start()
            return carry

        lax.fori_loop(0, NT, turn, 0)

    pl.run_scoped(
        transform,
        pltpu.VMEM((2 * BINS, SAMPLES), jnp.bfloat16),
        pltpu.VMEM((NW, NS, SAMPLES), jnp.bfloat16),
        pltpu.VMEM((2 * BINS * NW, NS), jnp.float32),
    )

    def wait_only(ref, sem):
        pltpu.make_async_copy(ref, ref, sem).wait()

    r_slot = jnp.where(col == y, 0, 2)
    lane = lax.broadcasted_iota(jnp.int32, (1, LANES), 1)
    scale = 1.0 / math.sqrt(WINDOWS)

    def rows_of(t, slot, src):
        parts = [buf[t, slot + c % 2, c // 2, src // 4, src % 4] for c in range(4)]
        return jnp.concatenate(parts, axis=0)

    def roll(tile, by):
        return pltpu.roll(tile.astype(jnp.float32), by, 1)

    def masked(tile, ahead, back, lo, hi):
        inside = (lane >= lo) & (lane < hi)
        turned = jnp.where(lane < lo + NW, ahead, -back).astype(jnp.bfloat16)
        zero = jnp.zeros_like(tile)
        return jnp.where(inside, tile, zero), jnp.where(inside, turned, zero)

    def main(lhs):
        def put(k, tile, ahead, back, lo, hi):
            plain, turned = masked(tile, ahead, back, lo, hi)
            lhs[pl.ds(0, 4 * NS), pl.ds(k * LANES, LANES)] = plain
            lhs[pl.ds(4 * NS, 4 * NS), pl.ds(k * LANES, LANES)] = turned

        def store(b, rhs):
            product = lax.dot_general(
                lhs[:, pl.ds(0, LANES * len(rhs))], jnp.concatenate(rhs, axis=1), NT_DIMS,
                preferred_element_type=jnp.float32,
            )
            product = (product * scale).astype(jnp.bfloat16)
            out_ref[0, b] = product[: 4 * NS]
            out_ref[1, b] = product[4 * NS :]

        def whole_bin(t, b):
            lo = 2 * NW * b - LANES * t
            for s in range(8):
                tile = rows_of(t, 0, s)
                put(s, tile, roll(tile, LANES - NW), roll(tile, NW), lo, lo + 2 * NW)
            store(b, [rows_of(t, r_slot, s) for s in range(8)])

        def split_bin(t, b):
            lo = 2 * NW * b - LANES * t
            for s in range(8):
                before, tile = rows_of(t - 1, 0, s), rows_of(t, 0, s)
                ahead = roll(tile, LANES - NW)
                back = roll(before, NW)
                put(2 * s, before, jnp.where(lane < LANES - NW, roll(before, LANES - NW), ahead),
                    back, lo + LANES, LANES)
                put(2 * s + 1, tile, ahead, jnp.where(lane < NW, back, roll(tile, NW)),
                    lo, lo + 2 * NW)
            store(b, [rows_of(t - 1 + i, r_slot, s) for s in range(8) for i in range(2)])

        def multiply(t):
            first = (LANES * t) // (2 * NW)
            last = (LANES * (t + 1)) // (2 * NW)
            split = (t % PERIOD != 0).astype(jnp.int32)

            @pl.when(t % PERIOD != 0)
            def _():
                split_bin(t, first)

            def one(b, carry):
                whole_bin(t, b)
                return carry

            lax.fori_loop(first + split, last, one, 0)

        def at(tau, lag):
            return jnp.logical_and(tau >= lag, tau < NT + lag)

        def step(tau, carry):
            @pl.when(tau < NT)
            def _():
                t = tau
                for c in own_copies(t):
                    c.wait()
                wait_only(buf.at[t, core, xl, xh, pl.ds(0, 3)], recvs.at[t, 0])
                wait_only(wbuf.at[t, pl.ds(0, 3)], recvs.at[t, 1])
                to_cross(t).start()
                to_twin_a(t).start()

                @pl.when(is_relay)
                def _():
                    relay_w_outer(t).start()

            @pl.when(at(tau, L1))
            def _():
                t = tau - L1
                to_cross(t).wait_recv()
                to_twin_b(t).start()

            @pl.when(at(tau, L2))
            def _():
                t = tau - L2
                to_twin_a(t).wait_recv()
                to_twin_b(t).wait_recv()

                @pl.when(is_source)
                def _():
                    source_outer_a(t).start()
                    source_outer_b(t).start()
                    source_pair(t).start()

                core_l(t).start()

            @pl.when(at(tau, L3))
            def _():
                t = tau - L3

                @pl.when(is_relay)
                def _():
                    source_outer_a(t).wait_recv()
                    relay_pair_a(t).start()
                    source_outer_b(t).wait_recv()
                    relay_pair_b(t).start()

                @pl.when(is_source)
                def _():
                    relay_w_outer(t).wait_recv()
                    source_w_pair(t).start()
                    source_cross_a(t).start()

            @pl.when(at(tau, L4))
            def _():
                t = tau - L4

                @pl.when(is_relay)
                def _():
                    relay_pair_a(t).wait_recv()
                    relay_outer(t).start()
                    relay_pair_b(t).wait_recv()

                @pl.when(is_source)
                def _():
                    source_w_pair(t).wait_recv()
                    source_cross_b(t).start()

            @pl.when(at(tau, L5))
            def _():
                t = tau - L5

                @pl.when(is_relay)
                def _():
                    source_cross_a(t).wait_recv()
                    source_cross_b(t).wait_recv()

                @pl.when(is_source)
                def _():
                    source_pair(t).wait_recv()
                    relay_outer(t).wait_recv()

                @pl.when(gives_r)
                def _():
                    core_r(t).start()

            @pl.when(tau >= L6)
            def _():
                t = tau - L6
                core_l(t).wait_recv()

                @pl.when(needs_r)
                def _():
                    core_r(t).wait_recv()

                multiply(t)

            return carry

        lax.fori_loop(0, NT + L6, step, 0)

    pl.run_scoped(main, pltpu.VMEM((8 * NS, 16 * LANES), jnp.bfloat16))

    def finish(t, carry):
        for c in z_copies(t) + [to_cross(t), to_twin_a(t), to_twin_b(t), core_l(t)]:
            c.wait_send()

        @pl.when(is_source)
        def _():
            for c in (source_pair, source_outer_a, source_outer_b, source_w_pair,
                      source_cross_a, source_cross_b):
                c(t).wait_send()

        @pl.when(is_relay)
        def _():
            for c in (relay_w_outer, relay_pair_a, relay_pair_b, relay_outer):
                c(t).wait_send()

        @pl.when(gives_r)
        def _():
            core_r(t).wait_send()

        return carry

    lax.fori_loop(0, NT, finish, 0)


def shards(traces, window_mask):
    dft = jnp.asarray(dft_table().astype(jnp.bfloat16))
    dma = pltpu.SemaphoreType.DMA
    bf16 = jnp.bfloat16
    return pl.pallas_call(
        kernel,
        out_shape=jax.ShapeDtypeStruct((2, 32, 320, 320), bf16),
        in_specs=[
            pl.BlockSpec(memory_space=pl.ANY),
            pl.BlockSpec(memory_space=pl.ANY),
            pl.BlockSpec(memory_space=pltpu.VMEM),
        ],
        out_specs=pl.BlockSpec(memory_space=pltpu.VMEM),
        scratch_shapes=[
            pltpu.VMEM((NT, 8, NS, LANES), bf16),
            pltpu.VMEM((NT, 4, NS, LANES), bf16),
            pltpu.VMEM((NT, 5, 2, 2, 4, NS, LANES), bf16),
            dma((CHUNKS + 1,)), dma((NT, 19)), dma((NT, 13)),
        ],
        compiler_params=pltpu.CompilerParams(
            collective_id=0, has_side_effects=True, vmem_limit_bytes=36 * 2**20
        ),
        cost_estimate=pl.CostEstimate(
            flops=12 * 10**9, bytes_accessed=20 * 10**6, transcendentals=0
        ),
        name="cross_spectra",
    )(dft, jnp.transpose(traces, (1, 0, 2)), jnp.transpose(window_mask))


def solution(mesh):
    placed = (P(("row", "col"), "freq", None), P(("row", "col"), "freq"))
    return jax.shard_map(
        shards, mesh=mesh, in_specs=placed, out_specs=P(None, "freq", "row", "col"), check_vma=False
    )
```

time: 429 us -> 130 us (0.30)
  waiting for transfers between devices: 208 us -> 0 us
  Pallas kernels: 0 us -> 120 us
  local copies, waits for them, and re-layouts: 83.9 us -> 9.22 us
  blocking collectives: 58.4 us -> 0 us
  other arithmetic: 32.1 us -> 0 us
  matrix products: 30.6 us -> 0 us
  between operations: 13.5 us -> 0.01 us
    all_gather x1 -> x0, waiting for transfers between devices: 208 us -> none  [shards(): everyone = lax.all_gather(regrouped, ('row', 'col'), axis=0, tiled=True)]
    pallas_call x0 -> x1, Pallas kernels: none -> 120 us  [shards(): pl.pallas_call(kernel, out_shape=jax.ShapeDtypeStruct((2, 32, 320, 320),...]
    all_to_all x1 -> x0, blocking collectives: 58.4 us -> none  [shards(): lax.all_to_all(whitened, 'freq', split_axis=1, concat_axis=2, tiled=True)]
    dynamic_slice x3 -> x0, local copies, waits for them, and re-layouts: 44.6 us -> none  [the longest x2 30.3 us: shards(): lax.dynamic_slice_in_dim(everyone, lax.axis_index('row') * block_rows, bl...]
    dot_general x2 -> x0, matrix products: 30.6 us -> none  [the longest x1 29.1 us: shards(): jnp.einsum('ifcw,jfdw->fcdij', left_side, right_side, preferred_element_t...]
    mul x3 -> x0, other arithmetic: 21.8 us -> none  [the longest x1 10.9 us: shards(): real_part = (products[:, 0, 0] + products[:, 1, 1]) * norm_scale]
    another operation x2 -> x0, local copies, waits for them, and re-layouts: 21.5 us -> none  [the longest x1 20.9 us: shards(): return jnp.stack([real_part, imag_part]).astype(jnp.bfloat16)]
    all_to_all x2 -> x0, local copies, waits for them, and re-layouts: 10.9 us -> none  [shards(): lax.all_to_all(whitened, 'freq', split_axis=1, concat_axis=2, tiled=True)]
  transfers between devices with their start and end apart: 1 -> 0, of which waited for: 1 -> 0; matrix products, arithmetic and copies ran while one was open for 0% -> 0% of each run, Pallas kernels for 0% -> 0%
where the time goes in v2:
time: 130 us; the launch traced here: 129 us
  Pallas kernels  120 us (92%)
  local copies, waits for them, and re-layouts  9.22 us (7%)
    pallas_call x1, Pallas kernels, shards(): pl.pallas_call(kernel, out_shape=jax.ShapeDtypeStruct((2, 32, 320, 320),...  120 us
    unnamed x7, local copies, waits for them, and re-layouts  9.22 us

profile of v2, /device:TPU:10, one launch (start us, length us, event | category | flops | bytes accessed | tf_op | source)
XLA Modules:
  0.0 129.3 jit_solution(702211310209328374)
XLA Ops:
  0.0 0.0 copy-start
  0.0 1.6 %copy-done = bf16[80,28,512]{2,0,1:T(8,128)(2,1)S(1)} copy-done((bf16[80,28,512]{2,0,1:T(8,128)(2,1)S(1)}, bf16[80,28,512]{2,0,1:T(8,128)(2,1)}, u32[]{:S(2)}) %copy-start) | copy-done | bytes 2293784
  1.6 0.0 copy-start.1
  1.6 0.7 copy-done.1
  2.4 0.0 copy-start.2
  2.4 1.0 copy-done.2
  3.4 120.1 %cross_spectra.1 = bf16[2,32,320,320]{3,2,1,0:T(8,128)(2,1)S(1)} custom-call(bf16[512,512]{1,0:T(8,128)(2,1)S(1)} %copy-done.2, bf16[28,80,512]{2,1,0:T(8,128)(2,1)S(1)} %bitcast.2, s32[28,80]{1,0:T(8,128)S(1)} %bitcast.3), custom_call_target="tpu_custom_call" | custom-call | flops 12000000000 | bytes 20000000 | tf_op jit(solution)/shard_map/cross_spectra/pallas_call | solution.py:400
  123.5 5.8 %copy.5 = bf16[2,32,320,320]{3,2,1,0:T(8,128)(2,1)} copy(bf16[2,32,320,320]{3,2,1,0:T(8,128)(2,1)S(1)} %cross_spectra.1) | data formatting | bytes 26214400
Async XLA Ops:
  0.0 1.6 %copy-start = (bf16[80,28,512]{2,0,1:T(8,128)(2,1)S(1)}, bf16[80,28,512]{2,0,1:T(8,128)(2,1)}, u32[]{:S(2)}) copy-start(bf16[80,28,512]{2,0,1:T(8,128)(2,1)} %param.3) | copy-start | bytes 6881284
  1.6 0.7 copy-start.1
  2.4 1.0 copy-start.2

commit v3 on v0

v3 whole, which is shorter than its diff:
```python
import math

import jax
import jax.numpy as jnp
import numpy as np
from jax import lax
from jax.experimental import pallas as pl
from jax.experimental.pallas import tpu as pltpu
from jax.sharding import PartitionSpec as P

SAMPLES = 512
BINS = 256
EPSILON = 1e-06
NS = 80
NW = 28
LANES = 128
NT = 14
PERIOD = 7
CHUNKS = 2
WINDOWS = 224
MESH = pl.DeviceIdType.MESH
NT_DIMS = (((1,), (1,)), ((), ()))

ORDER = (
    ("own", 0), ("turn", -3), ("loop_b", 5), ("relay_a", 1), ("twin_b", 1), ("send_a", 2),
    ("loop_a", 3), ("relay_b", 3), ("multiply", 7), ("send_b", 2), ("relay_c", 3), ("rows", 5),
)
Z, X1, CA, CB, CL, CR, O4, O1, O2, P4, P1, P2, XW = range(13)


def dft_table():
    t = np.arange(SAMPLES, dtype=np.int64)
    k = np.arange(BINS, dtype=np.int64)
    angles = 2.0 * math.pi / SAMPLES * ((k[:, None] * t[None, :]) % SAMPLES)
    taper = 0.5 - 0.5 * np.cos(2.0 * math.pi / SAMPLES * t)
    stacked = np.stack([taper * np.cos(angles), -taper * np.sin(angles)], axis=1)
    return stacked.reshape(2 * BINS, SAMPLES).astype(np.float32)


def kernel(
    dft_ref, traces_ref, mask_ref, out_ref, mine, wbuf, buf, sends, recvs,
):
    y = lax.axis_index("row")
    col = lax.axis_index("col")
    freq = lax.axis_index("freq")
    xl, core = col // 2, col % 2
    z, xh = freq // 2, freq % 2
    pair_y = y + 1 - 2 * (y % 2)
    outer_y = 3 - y
    far_y = 3 - pair_y
    is_source = (y // 2) == xl
    is_relay = jnp.logical_not(is_source)
    other_col = col + 1 - 2 * core
    x_col = (1 - xl) * 2 + core
    x_freq = z * 2 + 1 - xh

    others = [((z + k) % 4) for k in (1, 3, 2)]
    z_devs = [(y, col, o * 2 + xh) for o in others]
    twin = (y, x_col, freq)
    cross = (y, x_col, x_freq)
    pair = (pair_y, col, freq)
    outer = (outer_y, col, freq)
    mate = (y, other_col, freq)

    barrier = pltpu.get_barrier_semaphore()
    peers = z_devs + [twin, cross, pair, outer, mate]

    def remote(src, dst, send, recv, peer):
        return pltpu.make_async_remote_copy(
            src_ref=src, dst_ref=dst, send_sem=send, recv_sem=recv,
            device_id=peer, device_id_type=MESH,
        )

    def slot_of(row_, col_=col):
        return jnp.where(row_ == col_, 2 + core, 4)

    def free(t, row_, i):
        return buf.at[t, jnp.where(row_ == col, 2, 4), 0, i]

    def piece(t, slot, k):
        a, b = {1: (1 - xl, xh), 2: (xl, 1 - xh), 3: (1 - xl, 1 - xh), 4: (xl, xh)}[k]
        return buf.at[t, slot, a, b]

    def send(t, index, src, dst, recv, peer):
        return remote(src, dst, sends.at[index], recvs.at[t, recv], peer).start()

    def z_sends(t):
        for j in range(6):
            dst = wbuf.at[t, z] if j % 2 else buf.at[t, core, xl, xh, z]
            send(t, j, mine.at[t, j], dst, Z, z_devs[j // 2])

    needs_r = jnp.logical_not(col == y)
    gives_r = jnp.logical_not(other_col == y)

    def same(t, index, place, recv, peer):
        send(t, index, place, place, recv, peer)

    def transform(rows):
        for peer in peers:
            pl.semaphore_signal(barrier, inc=1, device_id=peer, device_id_type=MESH)

        def whiten(w, spectrum):
            energy = jnp.sum(spectrum * spectrum, axis=0, keepdims=True) * (1.0 / SAMPLES)
            factor = mask_ref[pl.ds(w, 1), :].astype(jnp.float32) * lax.rsqrt(energy + EPSILON)
            rows[pl.ds(w, 2 * BINS, stride=NW), :] = spectrum * factor

        def one_chunk(i, carry):
            for j in range(NW // CHUNKS // 2):
                w = i * (NW // CHUNKS) + 2 * j
                one, two = traces_ref[w], traces_ref[w + 1]
                spare = LANES - NS
                both = jnp.concatenate([one, two[:spare], two, one[:spare]], axis=0)
                spectrum = lax.dot_general(
                    dft_ref[...], both, NT_DIMS, preferred_element_type=jnp.float32
                )
                whiten(w, spectrum[:, :NS])
                whiten(w + 1, spectrum[:, LANES : LANES + NS])
            return carry

        lax.fori_loop(0, CHUNKS, one_chunk, 0)
        pl.semaphore_wait(barrier, len(peers))

    def wait_only(ref, sem):
        pltpu.make_async_copy(ref, ref, sem).wait()

    r_slot = jnp.where(col == y, 0, 2)
    lane = lax.broadcasted_iota(jnp.int32, (1, LANES), 1)
    scale = 1.0 / math.sqrt(WINDOWS)

    def rows_of(t, slot, src):
        parts = [buf[t, slot + c % 2, c // 2, src // 4, src % 4] for c in range(4)]
        return jnp.concatenate(parts, axis=0)

    def roll(tile, by):
        return pltpu.roll(tile.astype(jnp.float32), by, 1)

    def masked(tile, ahead, back, lo, hi):
        inside = (lane >= lo) & (lane < hi)
        turned = jnp.where(lane < lo + NW, ahead, -back).astype(jnp.bfloat16)
        zero = jnp.zeros_like(tile)
        return jnp.where(inside, tile, zero), jnp.where(inside, turned, zero)

    def main(rows, lhs):
        def turn(t):
            for k in range(4):
                for i in range(2):
                    f = ((z + (0, 1, 3, 2)[k]) % 4) * 2 + (1 - xh if i else xh)
                    start = pl.multiple_of((f * NT + t) * LANES, LANES)
                    turned = rows[pl.ds(start, LANES), :].T.astype(jnp.bfloat16)
                    if k:
                        mine[t, 2 * (k - 1) + i] = turned
                    elif i:
                        wbuf[t, z] = turned
                    else:
                        buf[t, core, xl, xh, z] = turned
            z_sends(t)

        def put(k, tile, ahead, back, lo, hi):
            plain, turned = masked(tile, ahead, back, lo, hi)
            lhs[pl.ds(0, 4 * NS), pl.ds(k * LANES, LANES)] = plain
            lhs[pl.ds(4 * NS, 4 * NS), pl.ds(k * LANES, LANES)] = turned

        def store(b, rhs):
            product = lax.dot_general(
                lhs[:, pl.ds(0, LANES * len(rhs))], jnp.concatenate(rhs, axis=1), NT_DIMS,
                preferred_element_type=jnp.float32,
            )
            product = (product * scale).astype(jnp.bfloat16)
            out_ref[0, b] = product[: 4 * NS]
            out_ref[1, b] = product[4 * NS :]

        def whole_bin(t, b):
            lo = 2 * NW * b - LANES * t
            for s in range(8):
                tile = rows_of(t, 0, s)
                put(s, tile, roll(tile, LANES - NW), roll(tile, NW), lo, lo + 2 * NW)
            store(b, [rows_of(t, r_slot, s) for s in range(8)])

        def split_bin(t, b):
            lo = 2 * NW * b - LANES * t
            for s in range(8):
                before, tile = rows_of(t - 1, 0, s), rows_of(t, 0, s)
                ahead = roll(tile, LANES - NW)
                back = roll(before, NW)
                put(2 * s, before, jnp.where(lane < LANES - NW, roll(before, LANES - NW), ahead),
                    back, lo + LANES, LANES)
                put(2 * s + 1, tile, ahead, jnp.where(lane < NW, back, roll(tile, NW)),
                    lo, lo + 2 * NW)
            store(b, [rows_of(t - 1 + i, r_slot, s) for s in range(8) for i in range(2)])

        def multiply(t):
            first = (LANES * t) // (2 * NW)
            last = (LANES * (t + 1)) // (2 * NW)
            split = (t % PERIOD != 0).astype(jnp.int32)

            @pl.when(t % PERIOD != 0)
            def _():
                split_bin(t, first)

            def one(b, carry):
                whole_bin(t, b)
                return carry

            lax.fori_loop(first + split, last, one, 0)

        def own(t):
            wait_only(mine.at[t], recvs.at[t, Z])
            send(t, 6, wbuf.at[t], piece(t, core, 4), X1, cross)
            same(t, 7, piece(t, core, 4), CA, twin)

            @pl.when(is_source)
            def _():
                send(t, 11, piece(t, core, 4), piece(t, slot_of(y), 4), O4, outer)

            @pl.when(is_relay)
            def _():
                send(t, 11, wbuf.at[t], free(t, outer_y, 0), O4, outer)

        def twin_b(t):
            wait_only(piece(t, core, 3), recvs.at[t, X1])
            same(t, 8, piece(t, core, 3), CB, twin)

            @pl.when(is_source)
            def _():
                send(t, 12, piece(t, core, 3), piece(t, slot_of(y), 3), P1, pair)

        def send_a(t):
            wait_only(piece(t, core, 1), recvs.at[t, CA])

            @pl.when(is_source)
            def _():
                send(t, 13, piece(t, core, 1), piece(t, slot_of(y), 1), O1, outer)
                send(t, 14, piece(t, core, 1), piece(t, slot_of(y), 1), P1, pair)

        def send_b(t):
            wait_only(piece(t, core, 2), recvs.at[t, CB])

            @pl.when(is_source)
            def _():
                send(t, 15, piece(t, core, 2), piece(t, slot_of(y), 2), O2, outer)

            same(t, 9, buf.at[t, core], CL, mate)

        def relay(t, index, k, recv, recv_next):
            held = piece(t, slot_of(outer_y), k)
            wait_only(held, recvs.at[t, recv])
            same(t, index, held, recv_next, pair)

        def relay_a(t):
            @pl.when(is_relay)
            def _():
                relay(t, 12, 4, O4, P4)

            @pl.when(is_source)
            def _():
                held = free(t, y, 0)
                wait_only(held, recvs.at[t, O4])
                send(t, 16, held, free(t, pair_y, 1), P4, pair)
                dst = buf.at[t, slot_of(outer_y, x_col), xl, xh]
                send(t, 17, held, dst, XW, cross)

        def relay_b(t):
            @pl.when(is_relay)
            def _():
                relay(t, 13, 1, O1, P1)

        def relay_c(t):
            @pl.when(is_relay)
            def _():
                relay(t, 14, 2, O2, P2)

        def loop_a(t):
            @pl.when(is_relay)
            def _():
                held = piece(t, slot_of(far_y), 4)
                wait_only(held, recvs.at[t, P4])
                same(t, 15, held, O1, outer)

            @pl.when(is_source)
            def _():
                held = free(t, y, 1)
                wait_only(held, recvs.at[t, P4])
                send(t, 18, held, buf.at[t, slot_of(far_y, x_col), xl, xh], XW, cross)

        def loop_b(t):
            @pl.when(is_relay)
            def _():
                held = piece(t, slot_of(far_y), 2)
                wait_only(held, recvs.at[t, P2])
                same(t, 16, held, O1, outer)
                wait_only(piece(t, slot_of(far_y), 1), recvs.at[t, P1])

        def both_rows(t):
            @pl.when(is_relay)
            def _():
                wait_only(buf.at[t, 4, xl], recvs.at[t, XW])

            @pl.when(is_source)
            def _():
                wait_only(buf.at[t, slot_of(pair_y), 1 - xl], recvs.at[t, P1])
                wait_only(buf.at[t, slot_of(pair_y), xl], recvs.at[t, O1])

            @pl.when(gives_r)
            def _():
                send(t, 10, buf.at[t, 4], buf.at[t, 2 + core], CR, mate)

        def products(t):
            wait_only(buf.at[t, 1 - core], recvs.at[t, CL])

            @pl.when(needs_r)
            def _():
                wait_only(buf.at[t, 3 - core], recvs.at[t, CR])

            multiply(t)

        events = {
            "own": own, "turn": turn, "loop_b": loop_b, "relay_a": relay_a, "twin_b": twin_b,
            "send_a": send_a, "loop_a": loop_a, "relay_b": relay_b, "multiply": products,
            "send_b": send_b, "relay_c": relay_c, "rows": both_rows,
        }

        def step(tau, carry):
            for name, lag in ORDER:
                @pl.when(jnp.logical_and(tau >= lag, tau < NT + lag))
                def _():
                    events[name](tau - lag)

            return carry

        for t in range(-dict(ORDER)["turn"]):
            turn(t)
        lax.fori_loop(0, NT + dict(ORDER)["multiply"], step, 0)

    def stages(rows):
        transform(rows)
        pl.run_scoped(
            lambda lhs: main(rows, lhs), pltpu.VMEM((8 * NS, 16 * LANES), jnp.bfloat16)
        )

    pl.run_scoped(stages, pltpu.VMEM((2 * BINS * NW, NS), jnp.float32))

    one, two = wbuf, buf.at[:, core]
    for j in range(6):
        wait_only(mine.at[:, j], sends.at[j])
    for j in (6, 7, 8, 11, 12, 13, 14, 15, 16):
        wait_only(one, sends.at[j])
    wait_only(two, sends.at[9])

    @pl.when(gives_r)
    def _():
        wait_only(two, sends.at[10])

    @pl.when(is_source)
    def _():
        for j in (17, 18):
            wait_only(one, sends.at[j])


def shards(traces, window_mask):
    dft = jnp.asarray(dft_table().astype(jnp.bfloat16))
    dma = pltpu.SemaphoreType.DMA
    bf16 = jnp.bfloat16
    return pl.pallas_call(
        kernel,
        out_shape=jax.ShapeDtypeStruct((2, 32, 320, 320), bf16),
        in_specs=[pl.BlockSpec(memory_space=pltpu.VMEM)] * 3,
        out_specs=pl.BlockSpec(memory_space=pltpu.VMEM),
        scratch_shapes=[
            pltpu.VMEM((NT, 6, NS, LANES), bf16),
            pltpu.VMEM((NT, 4, NS, LANES), bf16),
            pltpu.VMEM((NT, 5, 2, 2, 4, NS, LANES), bf16),
            dma((19,)), dma((NT, 13)),
        ],
        compiler_params=pltpu.CompilerParams(
            collective_id=0, has_side_effects=True, vmem_limit_bytes=36 * 2**20
        ),
        cost_estimate=pl.CostEstimate(
            flops=12 * 10**9, bytes_accessed=20 * 10**6, transcendentals=0
        ),
        name="cross_spectra",
    )(dft, jnp.transpose(traces, (1, 0, 2)), jnp.transpose(window_mask))


def solution(mesh):
    placed = (P(("row", "col"), "freq", None), P(("row", "col"), "freq"))
    return jax.shard_map(
        shards, mesh=mesh, in_specs=placed, out_specs=P(None, "freq", "row", "col"), check_vma=False
    )
```

time: 429 us -> 116 us (0.27)
  waiting for transfers between devices: 208 us -> 0 us
  Pallas kernels: 0 us -> 105 us
  local copies, waits for them, and re-layouts: 83.9 us -> 9.22 us
  blocking collectives: 58.4 us -> 0 us
  other arithmetic: 32.1 us -> 0 us
  matrix products: 30.6 us -> 0 us
  between operations: 13.5 us -> 0.01 us
    all_gather x1 -> x0, waiting for transfers between devices: 208 us -> none  [shards(): everyone = lax.all_gather(regrouped, ('row', 'col'), axis=0, tiled=True)]
    pallas_call x0 -> x1, Pallas kernels: none -> 105 us  [shards(): pl.pallas_call(kernel, out_shape=jax.ShapeDtypeStruct((2, 32, 320, 320),...]
    all_to_all x1 -> x0, blocking collectives: 58.4 us -> none  [shards(): lax.all_to_all(whitened, 'freq', split_axis=1, concat_axis=2, tiled=True)]
    dynamic_slice x3 -> x0, local copies, waits for them, and re-layouts: 44.6 us -> none  [the longest x2 30.3 us: shards(): lax.dynamic_slice_in_dim(everyone, lax.axis_index('row') * block_rows, bl...]
    dot_general x2 -> x0, matrix products: 30.6 us -> none  [the longest x1 29.1 us: shards(): jnp.einsum('ifcw,jfdw->fcdij', left_side, right_side, preferred_element_t...]
    mul x3 -> x0, other arithmetic: 21.8 us -> none  [the longest x1 10.9 us: shards(): real_part = (products[:, 0, 0] + products[:, 1, 1]) * norm_scale]
    another operation x2 -> x0, local copies, waits for them, and re-layouts: 21.5 us -> none  [the longest x1 20.9 us: shards(): return jnp.stack([real_part, imag_part]).astype(jnp.bfloat16)]
    all_to_all x2 -> x0, local copies, waits for them, and re-layouts: 10.9 us -> none  [shards(): lax.all_to_all(whitened, 'freq', split_axis=1, concat_axis=2, tiled=True)]
  transfers between devices with their start and end apart: 1 -> 0, of which waited for: 1 -> 0; matrix products, arithmetic and copies ran while one was open for 0% -> 0% of each run, Pallas kernels for 0% -> 0%
where the time goes in v3:
time: 116 us; the launch traced here: 115 us
  Pallas kernels  105 us (91%)
  local copies, waits for them, and re-layouts  9.22 us (8%)
    pallas_call x1, Pallas kernels, shards(): pl.pallas_call(kernel, out_shape=jax.ShapeDtypeStruct((2, 32, 320, 320),...  105 us
    unnamed x7, local copies, waits for them, and re-layouts  9.22 us

profile of v3, /device:TPU:10, one launch (start us, length us, event | category | flops | bytes accessed | tf_op | source)
XLA Modules:
  0.0 114.6 jit_solution(2420436756405505219)
XLA Ops:
  0.0 0.0 copy-start
  0.0 1.6 %copy-done = bf16[80,28,512]{2,0,1:T(8,128)(2,1)S(1)} copy-done((bf16[80,28,512]{2,0,1:T(8,128)(2,1)S(1)}, bf16[80,28,512]{2,0,1:T(8,128)(2,1)}, u32[]{:S(2)}) %copy-start) | copy-done | bytes 2293784
  1.6 0.0 copy-start.1
  1.6 0.7 copy-done.1
  2.4 0.0 copy-start.2
  2.4 1.0 copy-done.2
  3.4 105.4 %cross_spectra.1 = bf16[2,32,320,320]{3,2,1,0:T(8,128)(2,1)S(1)} custom-call(bf16[512,512]{1,0:T(8,128)(2,1)S(1)} %copy-done.2, bf16[28,80,512]{2,1,0:T(8,128)(2,1)S(1)} %bitcast.2, s32[28,80]{1,0:T(8,128)S(1)} %bitcast.3), custom_call_target="tpu_custom_call" | custom-call | flops 12000000000 | bytes 20000000 | tf_op jit(solution)/shard_map/cross_spectra/pallas_call | solution.py:363
  108.8 5.8 %copy.5 = bf16[2,32,320,320]{3,2,1,0:T(8,128)(2,1)} copy(bf16[2,32,320,320]{3,2,1,0:T(8,128)(2,1)S(1)} %cross_spectra.1) | data formatting | bytes 26214400
Async XLA Ops:
  0.0 1.6 %copy-start = (bf16[80,28,512]{2,0,1:T(8,128)(2,1)S(1)}, bf16[80,28,512]{2,0,1:T(8,128)(2,1)}, u32[]{:S(2)}) copy-start(bf16[80,28,512]{2,0,1:T(8,128)(2,1)} %param.3) | copy-start | bytes 6881284
  1.6 0.7 copy-start.1
  2.4 1.0 copy-start.2

commit v4 on v3

--- a/solution.py
+++ b/solution.py
@@ -131,14 +131,17 @@
         parts = [buf[t, slot + c % 2, c // 2, src // 4, src % 4] for c in range(4)]
         return jnp.concatenate(parts, axis=0)
 
-    def roll(tile, by):
-        return pltpu.roll(tile.astype(jnp.float32), by, 1)
-
-    def masked(tile, ahead, back, lo, hi):
-        inside = (lane >= lo) & (lane < hi)
-        turned = jnp.where(lane < lo + NW, ahead, -back).astype(jnp.bfloat16)
-        zero = jnp.zeros_like(tile)
-        return jnp.where(inside, tile, zero), jnp.where(inside, turned, zero)
+    def fold(t, slot, pair, lo, split):
+        tiles = []
+        for src in (2 * pair, 2 * pair + 1):
+            tile = rows_of(t, slot, src)
+            if split:
+                tile = jnp.where(lane >= lo + LANES, rows_of(t - 1, slot, src), tile)
+            tiles.append(tile)
+        return jnp.where(place(lo) < LANES // 2, tiles[0], pltpu.roll(tiles[1], LANES // 2, 1))
+
+    def place(lo):
+        return (lane - lo + LANES) % LANES
 
     def main(rows, lhs):
         def turn(t):
@@ -155,39 +158,26 @@
                         buf[t, core, xl, xh, z] = turned
             z_sends(t)
 
-        def put(k, tile, ahead, back, lo, hi):
-            plain, turned = masked(tile, ahead, back, lo, hi)
-            lhs[pl.ds(0, 4 * NS), pl.ds(k * LANES, LANES)] = plain
-            lhs[pl.ds(4 * NS, 4 * NS), pl.ds(k * LANES, LANES)] = turned
-
-        def store(b, rhs):
+        def one_bin(t, b, split):
+            lo = 2 * NW * b - LANES * t
+            half = place(lo) % (LANES // 2)
+            for pair in range(4):
+                tile = fold(t, 0, pair, lo, split)
+                ahead = pltpu.roll(tile, LANES - NW, 1)
+                back = pltpu.roll(tile, NW, 1)
+                turned = jnp.where(half < NW, ahead, -back)
+                zero = jnp.zeros_like(tile)
+                part = pl.ds(pair * LANES, LANES)
+                lhs[pl.ds(0, 4 * NS), part] = jnp.where(half < 2 * NW, tile, zero)
+                lhs[pl.ds(4 * NS, 4 * NS), part] = jnp.where(half < 2 * NW, turned, zero)
+            rhs = jnp.concatenate([fold(t, r_slot, pair, lo, split) for pair in range(4)], axis=1)
             product = lax.dot_general(
-                lhs[:, pl.ds(0, LANES * len(rhs))], jnp.concatenate(rhs, axis=1), NT_DIMS,
-                preferred_element_type=jnp.float32,
+                lhs[...], rhs, NT_DIMS, preferred_element_type=jnp.float32
             )
             product = (product * scale).astype(jnp.bfloat16)
             out_ref[0, b] = product[: 4 * NS]
             out_ref[1, b] = product[4 * NS :]
 
-        def whole_bin(t, b):
-            lo = 2 * NW * b - LANES * t
-            for s in range(8):
-                tile = rows_of(t, 0, s)
-                put(s, tile, roll(tile, LANES - NW), roll(tile, NW), lo, lo + 2 * NW)
-            store(b, [rows_of(t, r_slot, s) for s in range(8)])
-
-        def split_bin(t, b):
-            lo = 2 * NW * b - LANES * t
-            for s in range(8):
-                before, tile = rows_of(t - 1, 0, s), rows_of(t, 0, s)
-                ahead = roll(tile, LANES - NW)
-                back = roll(before, NW)
-                put(2 * s, before, jnp.where(lane < LANES - NW, roll(before, LANES - NW), ahead),
-                    back, lo + LANES, LANES)
-                put(2 * s + 1, tile, ahead, jnp.where(lane < NW, back, roll(tile, NW)),
-                    lo, lo + 2 * NW)
-            store(b, [rows_of(t - 1 + i, r_slot, s) for s in range(8) for i in range(2)])
-
         def multiply(t):
             first = (LANES * t) // (2 * NW)
             last = (LANES * (t + 1)) // (2 * NW)
@@ -195,10 +185,10 @@
 
             @pl.when(t % PERIOD != 0)
             def _():
-                split_bin(t, first)
+                one_bin(t, first, True)
 
             def one(b, carry):
-                whole_bin(t, b)
+                one_bin(t, b, False)
                 return carry
 
             lax.fori_loop(first + split, last, one, 0)
@@ -334,7 +324,7 @@
     def stages(rows):
         transform(rows)
         pl.run_scoped(
-            lambda lhs: main(rows, lhs), pltpu.VMEM((8 * NS, 16 * LANES), jnp.bfloat16)
+            lambda lhs: main(rows, lhs), pltpu.VMEM((8 * NS, 4 * LANES), jnp.bfloat16)
         )
 
     pl.run_scoped(stages, pltpu.VMEM((2 * BINS * NW, NS), jnp.float32))

time: 116 us -> 112 us (0.966)
  the two profiles are of different devices: /device:TPU:10 before, /device:TPU:1 now
where the time goes in v4:
time: 112 us
  Pallas kernels  103 us (92%)
  local copies, waits for them, and re-layouts  9.22 us (8%)
    pallas_call x1, Pallas kernels, shards(): pl.pallas_call(kernel, out_shape=jax.ShapeDtypeStruct((2, 32, 320, 320),...  103 us
    unnamed x7, local copies, waits for them, and re-layouts  9.22 us

profile of v4, /device:TPU:1, one launch (start us, length us, event | category | flops | bytes accessed | tf_op | source)
XLA Modules:
  0.0 112.0 jit_solution(2517536810177629090)
XLA Ops:
  0.0 0.0 copy-start
  0.0 1.6 %copy-done = bf16[80,28,512]{2,0,1:T(8,128)(2,1)S(1)} copy-done((bf16[80,28,512]{2,0,1:T(8,128)(2,1)S(1)}, bf16[80,28,512]{2,0,1:T(8,128)(2,1)}, u32[]{:S(2)}) %copy-start) | copy-done | bytes 2293784
  1.6 0.0 copy-start.1
  1.6 0.7 copy-done.1
  2.4 0.0 copy-start.2
  2.4 1.0 copy-done.2
  3.4 102.8 %cross_spectra.1 = bf16[2,32,320,320]{3,2,1,0:T(8,128)(2,1)S(1)} custom-call(bf16[512,512]{1,0:T(8,128)(2,1)S(1)} %copy-done.2, bf16[28,80,512]{2,1,0:T(8,128)(2,1)S(1)} %bitcast.2, s32[28,80]{1,0:T(8,128)S(1)} %bitcast.3), custom_call_target="tpu_custom_call" | custom-call | flops 12000000000 | bytes 20000000 | tf_op jit(solution)/shard_map/cross_spectra/pallas_call | solution.py:353
  106.2 5.8 %copy.5 = bf16[2,32,320,320]{3,2,1,0:T(8,128)(2,1)} copy(bf16[2,32,320,320]{3,2,1,0:T(8,128)(2,1)S(1)} %cross_spectra.1) | data formatting | bytes 26214400
Async XLA Ops:
  0.0 1.6 %copy-start = (bf16[80,28,512]{2,0,1:T(8,128)(2,1)S(1)}, bf16[80,28,512]{2,0,1:T(8,128)(2,1)}, u32[]{:S(2)}) copy-start(bf16[80,28,512]{2,0,1:T(8,128)(2,1)} %param.3) | copy-start | bytes 6881284
  1.6 0.7 copy-start.1
  2.4 1.0 copy-start.2

commit v5 on v4

--- a/solution.py
+++ b/solution.py
@@ -22,8 +22,25 @@
 NT_DIMS = (((1,), (1,)), ((), ()))
 
 ORDER = (
-    ("own", 0), ("turn", -3), ("loop_b", 5), ("relay_a", 1), ("twin_b", 1), ("send_a", 2),
-    ("loop_a", 3), ("relay_b", 3), ("multiply", 7), ("send_b", 2), ("relay_c", 3), ("rows", 5),
+    ("T", "own_t", 0),
+    ("S", "next_outer", 2),
+    ("S", "whole_s", 3),
+    ("T", "relay_4", 1),
+    ("T", "near_t", 1),
+    ("B", "products", 6),
+    ("T", "relay_1", 2),
+    ("T", "loop_1", 3),
+    ("B", "turn", -2),
+    ("T", "loop_4", 2),
+    ("S", "near_s", 2),
+    ("T", "twin_a_t", 1),
+    ("T", "whole_t", 3),
+    ("T", "relay_2", 3),
+    ("S", "own_s", 0),
+    ("S", "twin_a_s", 1),
+    ("S", "next_far", 3),
+    ("T", "rows_t", 4),
+    ("S", "rows_s", 4),
 )
 Z, X1, CA, CB, CL, CR, O4, O1, O2, P4, P1, P2, XW = range(13)
 
@@ -198,37 +215,40 @@
             send(t, 6, wbuf.at[t], piece(t, core, 4), X1, cross)
             same(t, 7, piece(t, core, 4), CA, twin)
 
-            @pl.when(is_source)
-            def _():
-                send(t, 11, piece(t, core, 4), piece(t, slot_of(y), 4), O4, outer)
-
-            @pl.when(is_relay)
-            def _():
-                send(t, 11, wbuf.at[t], free(t, outer_y, 0), O4, outer)
-
-        def twin_b(t):
+        def own_s(t):
+            own(t)
+            send(t, 11, piece(t, core, 4), piece(t, slot_of(y), 4), O4, outer)
+
+        def own_t(t):
+            own(t)
+            send(t, 11, wbuf.at[t], free(t, outer_y, 0), O4, outer)
+
+        def near(t):
             wait_only(piece(t, core, 3), recvs.at[t, X1])
             same(t, 8, piece(t, core, 3), CB, twin)
 
-            @pl.when(is_source)
-            def _():
-                send(t, 12, piece(t, core, 3), piece(t, slot_of(y), 3), P1, pair)
-
-        def send_a(t):
+        def near_s(t):
+            near(t)
+            send(t, 12, piece(t, core, 3), piece(t, slot_of(y), 3), P2, pair)
+
+        def twin_a(t):
             wait_only(piece(t, core, 1), recvs.at[t, CA])
 
-            @pl.when(is_source)
-            def _():
-                send(t, 13, piece(t, core, 1), piece(t, slot_of(y), 1), O1, outer)
-                send(t, 14, piece(t, core, 1), piece(t, slot_of(y), 1), P1, pair)
-
-        def send_b(t):
+        def twin_a_s(t):
+            twin_a(t)
+            send(t, 13, piece(t, core, 1), piece(t, slot_of(y), 1), O1, outer)
+
+        def whole(t):
             wait_only(piece(t, core, 2), recvs.at[t, CB])
 
-            @pl.when(is_source)
-            def _():
-                send(t, 15, piece(t, core, 2), piece(t, slot_of(y), 2), O2, outer)
-
+        def whole_s(t):
+            whole(t)
+            send(t, 15, piece(t, core, 2), piece(t, slot_of(y), 2), O2, outer)
+            send(t, 14, piece(t, core, 2), piece(t, slot_of(y), 2), P2, pair)
+            same(t, 9, buf.at[t, core], CL, mate)
+
+        def whole_t(t):
+            whole(t)
             same(t, 9, buf.at[t, core], CL, mate)
 
         def relay(t, index, k, recv, recv_next):
@@ -236,64 +256,52 @@
             wait_only(held, recvs.at[t, recv])
             same(t, index, held, recv_next, pair)
 
-        def relay_a(t):
-            @pl.when(is_relay)
-            def _():
-                relay(t, 12, 4, O4, P4)
-
-            @pl.when(is_source)
-            def _():
-                held = free(t, y, 0)
-                wait_only(held, recvs.at[t, O4])
-                send(t, 16, held, free(t, pair_y, 1), P4, pair)
-                dst = buf.at[t, slot_of(outer_y, x_col), xl, xh]
-                send(t, 17, held, dst, XW, cross)
-
-        def relay_b(t):
-            @pl.when(is_relay)
-            def _():
-                relay(t, 13, 1, O1, P1)
-
-        def relay_c(t):
-            @pl.when(is_relay)
-            def _():
-                relay(t, 14, 2, O2, P2)
-
-        def loop_a(t):
-            @pl.when(is_relay)
-            def _():
-                held = piece(t, slot_of(far_y), 4)
-                wait_only(held, recvs.at[t, P4])
-                same(t, 15, held, O1, outer)
-
-            @pl.when(is_source)
-            def _():
-                held = free(t, y, 1)
-                wait_only(held, recvs.at[t, P4])
-                send(t, 18, held, buf.at[t, slot_of(far_y, x_col), xl, xh], XW, cross)
-
-        def loop_b(t):
-            @pl.when(is_relay)
-            def _():
-                held = piece(t, slot_of(far_y), 2)
-                wait_only(held, recvs.at[t, P2])
-                same(t, 16, held, O1, outer)
-                wait_only(piece(t, slot_of(far_y), 1), recvs.at[t, P1])
-
-        def both_rows(t):
-            @pl.when(is_relay)
-            def _():
-                wait_only(buf.at[t, 4, xl], recvs.at[t, XW])
-
-            @pl.when(is_source)
-            def _():
-                wait_only(buf.at[t, slot_of(pair_y), 1 - xl], recvs.at[t, P1])
-                wait_only(buf.at[t, slot_of(pair_y), xl], recvs.at[t, O1])
-
+        def relay_4(t):
+            relay(t, 12, 4, O4, P4)
+
+        def relay_1(t):
+            relay(t, 13, 1, O1, P1)
+
+        def relay_2(t):
+            relay(t, 14, 2, O2, P2)
+
+        def next_outer(t):
+            held = free(t, y, 0)
+            wait_only(held, recvs.at[t, O4])
+            send(t, 16, held, free(t, pair_y, 1), P4, pair)
+            send(t, 17, held, buf.at[t, slot_of(outer_y, x_col), xl, xh], XW, cross)
+
+        def next_far(t):
+            held = free(t, y, 1)
+            wait_only(held, recvs.at[t, P4])
+            send(t, 18, held, buf.at[t, slot_of(far_y, x_col), xl, xh], XW, cross)
+
+        def loop(t, index, k, recv):
+            held = piece(t, slot_of(far_y), k)
+            wait_only(held, recvs.at[t, recv])
+            same(t, index, held, O1, outer)
+
+        def loop_4(t):
+            loop(t, 15, 4, P4)
+
+        def loop_1(t):
+            loop(t, 16, 1, P1)
+
+        def give(t):
             @pl.when(gives_r)
             def _():
                 send(t, 10, buf.at[t, 4], buf.at[t, 2 + core], CR, mate)
 
+        def rows_s(t):
+            wait_only(buf.at[t, 4, xl], recvs.at[t, P2])
+            wait_only(buf.at[t, 4, xl], recvs.at[t, O1])
+            give(t)
+
+        def rows_t(t):
+            wait_only(piece(t, slot_of(far_y), 2), recvs.at[t, P2])
+            wait_only(buf.at[t, 4, xl], recvs.at[t, XW])
+            give(t)
+
         def products(t):
             wait_only(buf.at[t, 1 - core], recvs.at[t, CL])
 
@@ -304,22 +312,30 @@
             multiply(t)
 
         events = {
-            "own": own, "turn": turn, "loop_b": loop_b, "relay_a": relay_a, "twin_b": twin_b,
-            "send_a": send_a, "loop_a": loop_a, "relay_b": relay_b, "multiply": products,
-            "send_b": send_b, "relay_c": relay_c, "rows": both_rows,
+            "turn": turn, "products": products,
+            "own_s": own_s, "near_s": near_s, "twin_a_s": twin_a_s, "whole_s": whole_s,
+            "next_outer": next_outer, "next_far": next_far, "rows_s": rows_s,
+            "own_t": own_t, "near_t": near, "twin_a_t": twin_a, "whole_t": whole_t,
+            "relay_4": relay_4, "relay_1": relay_1, "relay_2": relay_2,
+            "loop_4": loop_4, "loop_1": loop_1, "rows_t": rows_t,
         }
 
         def step(tau, carry):
-            for name, lag in ORDER:
-                @pl.when(jnp.logical_and(tau >= lag, tau < NT + lag))
+            for who, name, lag in ORDER:
+                run = jnp.logical_and(tau >= lag, tau < NT + lag)
+                if who != "B":
+                    run = jnp.logical_and(run, is_source if who == "S" else is_relay)
+
+                @pl.when(run)
                 def _():
                     events[name](tau - lag)
 
             return carry
 
-        for t in range(-dict(ORDER)["turn"]):
+        lags = {name: lag for _, name, lag in ORDER}
+        for t in range(-lags["turn"]):
             turn(t)
-        lax.fori_loop(0, NT + dict(ORDER)["multiply"], step, 0)
+        lax.fori_loop(0, NT + max(lags.values()), step, 0)
 
     def stages(rows):
         transform(rows)

time: 112 us -> 109 us (0.973)
  the two profiles are of different devices: /device:TPU:1 before, /device:TPU:10 now
where the time goes in v5:
time: 109 us
  Pallas kernels  99.6 us (91%)
  local copies, waits for them, and re-layouts  9.22 us (8%)
    pallas_call x1, Pallas kernels, shards(): pl.pallas_call(kernel, out_shape=jax.ShapeDtypeStruct((2, 32, 320, 320),...  99.6 us
    unnamed x7, local copies, waits for them, and re-layouts  9.22 us

profile of v5, /device:TPU:10, one launch (start us, length us, event | category | flops | bytes accessed | tf_op | source)
XLA Modules:
  0.0 108.8 jit_solution(13772059676394682933)
XLA Ops:
  0.0 0.0 copy-start
  0.0 1.6 %copy-done = bf16[80,28,512]{2,0,1:T(8,128)(2,1)S(1)} copy-done((bf16[80,28,512]{2,0,1:T(8,128)(2,1)S(1)}, bf16[80,28,512]{2,0,1:T(8,128)(2,1)}, u32[]{:S(2)}) %copy-start) | copy-done | bytes 2293784
  1.6 0.0 copy-start.1
  1.6 0.7 copy-done.1
  2.4 0.0 copy-start.2
  2.4 1.0 copy-done.2
  3.4 99.6 %cross_spectra.1 = bf16[2,32,320,320]{3,2,1,0:T(8,128)(2,1)S(1)} custom-call(bf16[512,512]{1,0:T(8,128)(2,1)S(1)} %copy-done.2, bf16[28,80,512]{2,1,0:T(8,128)(2,1)S(1)} %bitcast.2, s32[28,80]{1,0:T(8,128)S(1)} %bitcast.3), custom_call_target="tpu_custom_call" | custom-call | flops 12000000000 | bytes 20000000 | tf_op jit(solution)/shard_map/cross_spectra/pallas_call | solution.py:369
  103.0 5.8 %copy.5 = bf16[2,32,320,320]{3,2,1,0:T(8,128)(2,1)} copy(bf16[2,32,320,320]{3,2,1,0:T(8,128)(2,1)S(1)} %cross_spectra.1) | data formatting | bytes 26214400
Async XLA Ops:
  0.0 1.6 %copy-start = (bf16[80,28,512]{2,0,1:T(8,128)(2,1)S(1)}, bf16[80,28,512]{2,0,1:T(8,128)(2,1)}, u32[]{:S(2)}) copy-start(bf16[80,28,512]{2,0,1:T(8,128)(2,1)} %param.3) | copy-start | bytes 6881284
  1.6 0.7 copy-start.1
  2.4 1.0 copy-start.2

commit v6 on v5

--- a/solution.py
+++ b/solution.py
@@ -1,3 +1,4 @@
+import functools
 import math
 
 import jax
@@ -55,7 +56,7 @@
 
 
 def kernel(
-    dft_ref, traces_ref, mask_ref, out_ref, mine, wbuf, buf, sends, recvs,
+    dft_hbm, traces_hbm, mask_hbm, out_ref, mine, wbuf, buf, inputs, sends, recvs,
 ):
     y = lax.axis_index("row")
     col = lax.axis_index("col")
@@ -112,7 +113,19 @@
     def same(t, index, place, recv, peer):
         send(t, index, place, place, recv, peer)
 
-    def transform(rows):
+    def transform(rows, dft_ref, traces_ref, mask_ref):
+        per = NW // CHUNKS
+        table = pltpu.make_async_copy(dft_hbm, dft_ref, inputs.at[CHUNKS])
+        masks = pltpu.make_async_copy(mask_hbm, mask_ref, inputs.at[CHUNKS + 1])
+
+        def chunk(i):
+            part = pl.ds(i * per, per)
+            return pltpu.make_async_copy(traces_hbm.at[part], traces_ref.at[part], inputs.at[i])
+
+        table.start()
+        masks.start()
+        for i in range(CHUNKS):
+            chunk(i).start()
         for peer in peers:
             pl.semaphore_signal(barrier, inc=1, device_id=peer, device_id_type=MESH)
 
@@ -122,8 +135,9 @@
             rows[pl.ds(w, 2 * BINS, stride=NW), :] = spectrum * factor
 
         def one_chunk(i, carry):
-            for j in range(NW // CHUNKS // 2):
-                w = i * (NW // CHUNKS) + 2 * j
+            chunk(i).wait()
+            for j in range(per // 2):
+                w = i * per + 2 * j
                 one, two = traces_ref[w], traces_ref[w + 1]
                 spare = LANES - NS
                 both = jnp.concatenate([one, two[:spare], two, one[:spare]], axis=0)
@@ -134,6 +148,8 @@
                 whiten(w + 1, spectrum[:, LANES : LANES + NS])
             return carry
 
+        table.wait()
+        masks.wait()
         lax.fori_loop(0, CHUNKS, one_chunk, 0)
         pl.semaphore_wait(barrier, len(peers))
 
@@ -338,7 +354,12 @@
         lax.fori_loop(0, NT + max(lags.values()), step, 0)
 
     def stages(rows):
-        transform(rows)
+        pl.run_scoped(
+            functools.partial(transform, rows),
+            pltpu.VMEM((2 * BINS, SAMPLES), jnp.bfloat16),
+            pltpu.VMEM((NW, NS, SAMPLES), jnp.bfloat16),
+            pltpu.VMEM((NW, NS), jnp.int32),
+        )
         pl.run_scoped(
             lambda lhs: main(rows, lhs), pltpu.VMEM((8 * NS, 4 * LANES), jnp.bfloat16)
         )
@@ -360,6 +381,10 @@
     def _():
         for j in (17, 18):
             wait_only(one, sends.at[j])
+
+
+def hbm(array):
+    return pltpu.with_memory_space_constraint(array, pltpu.HBM)
 
 
 def shards(traces, window_mask):
@@ -369,13 +394,13 @@
     return pl.pallas_call(
         kernel,
         out_shape=jax.ShapeDtypeStruct((2, 32, 320, 320), bf16),
-        in_specs=[pl.BlockSpec(memory_space=pltpu.VMEM)] * 3,
+        in_specs=[pl.BlockSpec(memory_space=pltpu.HBM)] * 3,
         out_specs=pl.BlockSpec(memory_space=pltpu.VMEM),
         scratch_shapes=[
             pltpu.VMEM((NT, 6, NS, LANES), bf16),
             pltpu.VMEM((NT, 4, NS, LANES), bf16),
             pltpu.VMEM((NT, 5, 2, 2, 4, NS, LANES), bf16),
-            dma((19,)), dma((NT, 13)),
+            dma((CHUNKS + 2,)), dma((19,)), dma((NT, 13)),
         ],
         compiler_params=pltpu.CompilerParams(
             collective_id=0, has_side_effects=True, vmem_limit_bytes=36 * 2**20
@@ -384,7 +409,7 @@
             flops=12 * 10**9, bytes_accessed=20 * 10**6, transcendentals=0
         ),
         name="cross_spectra",
-    )(dft, jnp.transpose(traces, (1, 0, 2)), jnp.transpose(window_mask))
+    )(hbm(dft), hbm(jnp.transpose(traces, (1, 0, 2))), hbm(jnp.transpose(window_mask)))
 
 
 def solution(mesh):

time: 109 us -> 107 us (0.982)
  local copies, waits for them, and re-layouts: 9.22 us -> 5.81 us
  Pallas kernels: 99.6 us -> 101 us
    unnamed x7 -> x1, local copies, waits for them, and re-layouts: 9.22 us -> 5.81 us
    pallas_call x1, Pallas kernels: 99.6 us -> 101 us  [shards(): pl.pallas_call(kernel, out_shape=jax.ShapeDtypeStruct((2, 32, 320, 320),...]
where the time goes in v6:
time: 107 us
  Pallas kernels  101 us (94%)
  local copies, waits for them, and re-layouts  5.81 us (5%)
    pallas_call x1, Pallas kernels, shards(): pl.pallas_call(kernel, out_shape=jax.ShapeDtypeStruct((2, 32, 320, 320),...  101 us
    unnamed x1, local copies, waits for them, and re-layouts  5.81 us

profile of v6, /device:TPU:10, one launch (start us, length us, event | category | flops | bytes accessed | tf_op | source)
XLA Modules:
  0.0 106.9 jit_solution(15901913398997552204)
XLA Ops:
  0.0 101.1 %cross_spectra.1 = bf16[2,32,320,320]{3,2,1,0:T(8,128)(2,1)S(1)} custom-call(bf16[512,512]{1,0:T(8,128)(2,1)} %constant.2.clone.dft_hbm, bf16[28,80,512]{2,1,0:T(8,128)(2,1)} %bitcast.2, s32[28,80]{1,0:T(8,128)} %bitcast.3), custom_call_target="tpu_custom_call" | custom-call | flops 12000000000 | bytes 20000000 | tf_op jit(solution)/shard_map/cross_spectra/pallas_call | solution.py:394
  101.1 5.8 %copy.5 = bf16[2,32,320,320]{3,2,1,0:T(8,128)(2,1)} copy(bf16[2,32,320,320]{3,2,1,0:T(8,128)(2,1)S(1)} %cross_spectra.1) | data formatting | bytes 26214400

commit v7 on v6

--- a/solution.py
+++ b/solution.py
@@ -17,6 +17,7 @@
 LANES = 128
 NT = 14
 PERIOD = 7
+RING = 8
 CHUNKS = 2
 WINDOWS = 224
 MESH = pl.DeviceIdType.MESH
@@ -100,7 +101,7 @@
         return buf.at[t, slot, a, b]
 
     def send(t, index, src, dst, recv, peer):
-        return remote(src, dst, sends.at[index], recvs.at[t, recv], peer).start()
+        return remote(src, dst, sends.at[index], recvs.at[t % RING, recv], peer).start()
 
     def z_sends(t):
         for j in range(6):
@@ -227,7 +228,7 @@
             lax.fori_loop(first + split, last, one, 0)
 
         def own(t):
-            wait_only(mine.at[t], recvs.at[t, Z])
+            wait_only(mine.at[t], recvs.at[t % RING, Z])
             send(t, 6, wbuf.at[t], piece(t, core, 4), X1, cross)
             same(t, 7, piece(t, core, 4), CA, twin)
 
@@ -240,7 +241,7 @@
             send(t, 11, wbuf.at[t], free(t, outer_y, 0), O4, outer)
 
         def near(t):
-            wait_only(piece(t, core, 3), recvs.at[t, X1])
+            wait_only(piece(t, core, 3), recvs.at[t % RING, X1])
             same(t, 8, piece(t, core, 3), CB, twin)
 
         def near_s(t):
@@ -248,14 +249,14 @@
             send(t, 12, piece(t, core, 3), piece(t, slot_of(y), 3), P2, pair)
 
         def twin_a(t):
-            wait_only(piece(t, core, 1), recvs.at[t, CA])
+            wait_only(piece(t, core, 1), recvs.at[t % RING, CA])
 
         def twin_a_s(t):
             twin_a(t)
             send(t, 13, piece(t, core, 1), piece(t, slot_of(y), 1), O1, outer)
 
         def whole(t):
-            wait_only(piece(t, core, 2), recvs.at[t, CB])
+            wait_only(piece(t, core, 2), recvs.at[t % RING, CB])
 
         def whole_s(t):
             whole(t)
@@ -269,7 +270,7 @@
 
         def relay(t, index, k, recv, recv_next):
             held = piece(t, slot_of(outer_y), k)
-            wait_only(held, recvs.at[t, recv])
+            wait_only(held, recvs.at[t % RING, recv])
             same(t, index, held, recv_next, pair)
 
         def relay_4(t):
@@ -283,18 +284,18 @@
 
         def next_outer(t):
             held = free(t, y, 0)
-            wait_only(held, recvs.at[t, O4])
+            wait_only(held, recvs.at[t % RING, O4])
             send(t, 16, held, free(t, pair_y, 1), P4, pair)
             send(t, 17, held, buf.at[t, slot_of(outer_y, x_col), xl, xh], XW, cross)
 
         def next_far(t):
             held = free(t, y, 1)
-            wait_only(held, recvs.at[t, P4])
+            wait_only(held, recvs.at[t % RING, P4])
             send(t, 18, held, buf.at[t, slot_of(far_y, x_col), xl, xh], XW, cross)
 
         def loop(t, index, k, recv):
             held = piece(t, slot_of(far_y), k)
-            wait_only(held, recvs.at[t, recv])
+            wait_only(held, recvs.at[t % RING, recv])
             same(t, index, held, O1, outer)
 
         def loop_4(t):
@@ -309,21 +310,21 @@
                 send(t, 10, buf.at[t, 4], buf.at[t, 2 + core], CR, mate)
 
         def rows_s(t):
-            wait_only(buf.at[t, 4, xl], recvs.at[t, P2])
-            wait_only(buf.at[t, 4, xl], recvs.at[t, O1])
+            wait_only(buf.at[t, 4, xl], recvs.at[t % RING, P2])
+            wait_only(buf.at[t, 4, xl], recvs.at[t % RING, O1])
             give(t)
 
         def rows_t(t):
-            wait_only(piece(t, slot_of(far_y), 2), recvs.at[t, P2])
-            wait_only(buf.at[t, 4, xl], recvs.at[t, XW])
+            wait_only(piece(t, slot_of(far_y), 2), recvs.at[t % RING, P2])
+            wait_only(buf.at[t, 4, xl], recvs.at[t % RING, XW])
             give(t)
 
         def products(t):
-            wait_only(buf.at[t, 1 - core], recvs.at[t, CL])
+            wait_only(buf.at[t, 1 - core], recvs.at[t % RING, CL])
 
             @pl.when(needs_r)
             def _():
-                wait_only(buf.at[t, 3 - core], recvs.at[t, CR])
+                wait_only(buf.at[t, 3 - core], recvs.at[t % RING, CR])
 
             multiply(t)
 
@@ -400,7 +401,7 @@
             pltpu.VMEM((NT, 6, NS, LANES), bf16),
             pltpu.VMEM((NT, 4, NS, LANES), bf16),
             pltpu.VMEM((NT, 5, 2, 2, 4, NS, LANES), bf16),
-            dma((CHUNKS + 2,)), dma((19,)), dma((NT, 13)),
+            dma((CHUNKS + 2,)), dma((19,)), dma((RING, 13)),
         ],
         compiler_params=pltpu.CompilerParams(
             collective_id=0, has_side_effects=True, vmem_limit_bytes=36 * 2**20

time: 107 us -> 107 us (level)
  no operation moved by 1% of the time
where the time goes in v7:
time: 107 us; the launch traced here: 106 us
  Pallas kernels  100 us (93%)
  local copies, waits for them, and re-layouts  5.81 us (5%)
    pallas_call x1, Pallas kernels, shards(): pl.pallas_call(kernel, out_shape=jax.ShapeDtypeStruct((2, 32, 320, 320),...  100 us
    unnamed x1, local copies, waits for them, and re-layouts  5.81 us

profile of v7, /device:TPU:10, one launch (start us, length us, event | category | flops | bytes accessed | tf_op | source)
XLA Modules:
  0.0 106.2 jit_solution(12434300510046448555)
XLA Ops:
  0.0 100.4 %cross_spectra.1 = bf16[2,32,320,320]{3,2,1,0:T(8,128)(2,1)S(1)} custom-call(bf16[512,512]{1,0:T(8,128)(2,1)} %constant.2.clone.dft_hbm, bf16[28,80,512]{2,1,0:T(8,128)(2,1)} %bitcast.2, s32[28,80]{1,0:T(8,128)} %bitcast.3), custom_call_target="tpu_custom_call" | custom-call | flops 12000000000 | bytes 20000000 | tf_op jit(solution)/shard_map/cross_spectra/pallas_call | solution.py:395
  100.4 5.8 %copy.5 = bf16[2,32,320,320]{3,2,1,0:T(8,128)(2,1)} copy(bf16[2,32,320,320]{3,2,1,0:T(8,128)(2,1)S(1)} %cross_spectra.1) | data formatting | bytes 26214400

commit v8 on v7

--- a/solution.py
+++ b/solution.py
@@ -17,6 +17,9 @@
 LANES = 128
 NT = 14
 PERIOD = 7
+TAIL = 2
+BEGUN = LANES * (NT - TAIL) // (2 * NW)
+PARTS = 3
 RING = 8
 CHUNKS = 2
 WINDOWS = 224
@@ -56,8 +59,65 @@
     return stacked.reshape(2 * BINS, SAMPLES).astype(np.float32)
 
 
+def products_of(buf, lhs, r_slot, put):
+    lane = lax.broadcasted_iota(jnp.int32, (1, LANES), 1)
+    scale = 1.0 / math.sqrt(WINDOWS)
+
+    def rows_of(t, slot, src):
+        parts = [buf[t, slot + c % 2, c // 2, src // 4, src % 4] for c in range(4)]
+        return jnp.concatenate(parts, axis=0)
+
+    def fold(t, slot, pair, lo, split):
+        tiles = []
+        for src in (2 * pair, 2 * pair + 1):
+            tile = rows_of(t, slot, src)
+            if split:
+                tile = jnp.where(lane >= lo + LANES, rows_of(t - 1, slot, src), tile)
+            tiles.append(tile)
+        return jnp.where(place(lo) < LANES // 2, tiles[0], pltpu.roll(tiles[1], LANES // 2, 1))
+
+    def place(lo):
+        return (lane - lo + LANES) % LANES
+
+    def one_bin(t, b, split):
+        lo = 2 * NW * b - LANES * t
+        half = place(lo) % (LANES // 2)
+        for pair in range(4):
+            tile = fold(t, 0, pair, lo, split)
+            ahead = pltpu.roll(tile, LANES - NW, 1)
+            back = pltpu.roll(tile, NW, 1)
+            turned = jnp.where(half < NW, ahead, -back)
+            zero = jnp.zeros_like(tile)
+            part = pl.ds(pair * LANES, LANES)
+            lhs[pl.ds(0, 4 * NS), part] = jnp.where(half < 2 * NW, tile, zero)
+            lhs[pl.ds(4 * NS, 4 * NS), part] = jnp.where(half < 2 * NW, turned, zero)
+        rhs = jnp.concatenate([fold(t, r_slot, pair, lo, split) for pair in range(4)], axis=1)
+        product = lax.dot_general(
+            lhs[...], rhs, NT_DIMS, preferred_element_type=jnp.float32
+        )
+        product = (product * scale).astype(jnp.bfloat16)
+        put(b, product[: 4 * NS], product[4 * NS :])
+
+    def multiply(t):
+        first = (LANES * t) // (2 * NW)
+        last = (LANES * (t + 1)) // (2 * NW)
+        split = (t % PERIOD != 0).astype(jnp.int32)
+
+        @pl.when(t % PERIOD != 0)
+        def _():
+            one_bin(t, first, True)
+
+        def one(b, carry):
+            one_bin(t, b, False)
+            return carry
+
+        lax.fori_loop(first + split, last, one, 0)
+
+    return multiply
+
+
 def kernel(
-    dft_hbm, traces_hbm, mask_hbm, out_ref, mine, wbuf, buf, inputs, sends, recvs,
+    dft_hbm, traces_hbm, mask_hbm, out_ref, buf, mine, wbuf, inputs, sends, recvs,
 ):
     y = lax.axis_index("row")
     col = lax.axis_index("col")
@@ -157,26 +217,6 @@
     def wait_only(ref, sem):
         pltpu.make_async_copy(ref, ref, sem).wait()
 
-    r_slot = jnp.where(col == y, 0, 2)
-    lane = lax.broadcasted_iota(jnp.int32, (1, LANES), 1)
-    scale = 1.0 / math.sqrt(WINDOWS)
-
-    def rows_of(t, slot, src):
-        parts = [buf[t, slot + c % 2, c // 2, src // 4, src % 4] for c in range(4)]
-        return jnp.concatenate(parts, axis=0)
-
-    def fold(t, slot, pair, lo, split):
-        tiles = []
-        for src in (2 * pair, 2 * pair + 1):
-            tile = rows_of(t, slot, src)
-            if split:
-                tile = jnp.where(lane >= lo + LANES, rows_of(t - 1, slot, src), tile)
-            tiles.append(tile)
-        return jnp.where(place(lo) < LANES // 2, tiles[0], pltpu.roll(tiles[1], LANES // 2, 1))
-
-    def place(lo):
-        return (lane - lo + LANES) % LANES
-
     def main(rows, lhs):
         def turn(t):
             for k in range(4):
@@ -192,40 +232,11 @@
                         buf[t, core, xl, xh, z] = turned
             z_sends(t)
 
-        def one_bin(t, b, split):
-            lo = 2 * NW * b - LANES * t
-            half = place(lo) % (LANES // 2)
-            for pair in range(4):
-                tile = fold(t, 0, pair, lo, split)
-                ahead = pltpu.roll(tile, LANES - NW, 1)
-                back = pltpu.roll(tile, NW, 1)
-                turned = jnp.where(half < NW, ahead, -back)
-                zero = jnp.zeros_like(tile)
-                part = pl.ds(pair * LANES, LANES)
-                lhs[pl.ds(0, 4 * NS), part] = jnp.where(half < 2 * NW, tile, zero)
-                lhs[pl.ds(4 * NS, 4 * NS), part] = jnp.where(half < 2 * NW, turned, zero)
-            rhs = jnp.concatenate([fold(t, r_slot, pair, lo, split) for pair in range(4)], axis=1)
-            product = lax.dot_general(
-                lhs[...], rhs, NT_DIMS, preferred_element_type=jnp.float32
-            )
-            product = (product * scale).astype(jnp.bfloat16)
-            out_ref[0, b] = product[: 4 * NS]
-            out_ref[1, b] = product[4 * NS :]
-
-        def multiply(t):
-            first = (LANES * t) // (2 * NW)
-            last = (LANES * (t + 1)) // (2 * NW)
-            split = (t % PERIOD != 0).astype(jnp.int32)
-
-            @pl.when(t % PERIOD != 0)
-            def _():
-                one_bin(t, first, True)
-
-            def one(b, carry):
-                one_bin(t, b, False)
-                return carry
-
-            lax.fori_loop(first + split, last, one, 0)
+        def put(b, real, imag):
+            out_ref[0, b] = real
+            out_ref[1, b] = imag
+
+        multiply = products_of(buf, lhs, jnp.where(col == y, 0, 2), put)
 
         def own(t):
             wait_only(mine.at[t], recvs.at[t % RING, Z])
@@ -326,7 +337,9 @@
             def _():
                 wait_only(buf.at[t, 3 - core], recvs.at[t % RING, CR])
 
-            multiply(t)
+            @pl.when(t < NT - TAIL)
+            def _():
+                multiply(t)
 
         events = {
             "turn": turn, "products": products,
@@ -384,6 +397,36 @@
             wait_only(one, sends.at[j])
 
 
+def finish_kernel(begun, buf, out_hbm, lhs, last, sems):
+    per = BEGUN // PARTS
+    copies = []
+    for c in range(2):
+        for i in range(PARTS):
+            part = pl.ds(i * per, per)
+            copies.append(
+                pltpu.make_async_copy(begun.at[c, part], out_hbm.at[c, part], sems.at[c, i])
+            )
+    for copy in copies:
+        copy.start()
+
+    def put(b, real, imag):
+        last[0, b - BEGUN] = real
+        last[1, b - BEGUN] = imag
+
+    row_is_col = lax.axis_index("row") == lax.axis_index("col")
+    multiply = products_of(buf, lhs, jnp.where(row_is_col, 0, 2), put)
+    for t in range(NT - TAIL, NT):
+        multiply(jnp.int32(t))
+    for c in range(2):
+        copy = pltpu.make_async_copy(
+            last.at[c], out_hbm.at[c, pl.ds(BEGUN, 32 - BEGUN)], sems.at[c, PARTS]
+        )
+        copy.start()
+        copies.append(copy)
+    for copy in copies:
+        copy.wait()
+
+
 def hbm(array):
     return pltpu.with_memory_space_constraint(array, pltpu.HBM)
 
@@ -392,25 +435,41 @@
     dft = jnp.asarray(dft_table().astype(jnp.bfloat16))
     dma = pltpu.SemaphoreType.DMA
     bf16 = jnp.bfloat16
-    return pl.pallas_call(
+    begun, spectra = pl.pallas_call(
         kernel,
-        out_shape=jax.ShapeDtypeStruct((2, 32, 320, 320), bf16),
+        out_shape=[
+            jax.ShapeDtypeStruct((2, BEGUN, 320, 320), bf16),
+            jax.ShapeDtypeStruct((NT, 5, 2, 2, 4, NS, LANES), bf16),
+        ],
         in_specs=[pl.BlockSpec(memory_space=pltpu.HBM)] * 3,
-        out_specs=pl.BlockSpec(memory_space=pltpu.VMEM),
+        out_specs=[pl.BlockSpec(memory_space=pltpu.VMEM)] * 2,
         scratch_shapes=[
             pltpu.VMEM((NT, 6, NS, LANES), bf16),
             pltpu.VMEM((NT, 4, NS, LANES), bf16),
-            pltpu.VMEM((NT, 5, 2, 2, 4, NS, LANES), bf16),
             dma((CHUNKS + 2,)), dma((19,)), dma((RING, 13)),
         ],
         compiler_params=pltpu.CompilerParams(
-            collective_id=0, has_side_effects=True, vmem_limit_bytes=36 * 2**20
+            collective_id=0, has_side_effects=True, vmem_limit_bytes=14 * 2**20
         ),
         cost_estimate=pl.CostEstimate(
             flops=12 * 10**9, bytes_accessed=20 * 10**6, transcendentals=0
         ),
         name="cross_spectra",
     )(hbm(dft), hbm(jnp.transpose(traces, (1, 0, 2))), hbm(jnp.transpose(window_mask)))
+    ended = 32 - BEGUN
+    return pl.pallas_call(
+        finish_kernel,
+        out_shape=jax.ShapeDtypeStruct((2, 32, 320, 320), bf16),
+        in_specs=[pl.BlockSpec(memory_space=pltpu.VMEM)] * 2,
+        out_specs=pl.BlockSpec(memory_space=pltpu.HBM),
+        scratch_shapes=[
+            pltpu.VMEM((8 * NS, 4 * LANES), bf16),
+            pltpu.VMEM((2, ended, 320, 320), bf16),
+            dma((2, PARTS + 1)),
+        ],
+        compiler_params=pltpu.CompilerParams(vmem_limit_bytes=12 * 2**20),
+        name="finish",
+    )(begun, spectra)
 
 
 def solution(mesh):

time: 107 us -> 104 us (0.972)
  local copies, waits for them, and re-layouts: 5.81 us -> 0 us
  Pallas kernels: 100 us -> 104 us
    unnamed x1 -> x0, local copies, waits for them, and re-layouts: 5.81 us -> none
    pallas_call x1 -> x2, Pallas kernels: 100 us -> 104 us  [the longest x1 98.1 us: shards(): pl.pallas_call(kernel, out_shape=[jax.ShapeDtypeStruct((2, BEGUN, 320, 32...]
where the time goes in v8:
time: 104 us
  Pallas kernels  104 us (100%)
    pallas_call x1, Pallas kernels, shards(): pl.pallas_call(kernel, out_shape=[jax.ShapeDtypeStruct((2, BEGUN, 320, 32...  98.1 us
    pallas_call x1, Pallas kernels, shards(): pl.pallas_call(finish_kernel, out_shape=jax.ShapeDtypeStruct((2, 32, 320,...  5.6 us

profile of v8, /device:TPU:10, one launch (start us, length us, event | category | flops | bytes accessed | tf_op | source)
XLA Modules:
  0.0 103.7 jit_solution(16098252186044490578)
XLA Ops:
  0.0 98.1 %cross_spectra.1 = (bf16[2,27,320,320]{3,2,1,0:T(8,128)(2,1)S(1)}, bf16[14,5,2,2,4,80,128]{6,5,4,3,2,1,0:T(8,128)(2,1)S(1)}) custom-call(bf16[512,512]{1,0:T(8,128)(2,1)} %constant.2.clone.dft_hbm, bf16[28,80,512]{2,1,0:T(8,128)(2,1)} %bitcast.2, s32[28,80]{1,0:T(8,128)} %bitcast.3), custom_call_target="tpu_custom_call" | custom-call | flops 12000000000 | bytes 20000000 | tf_op jit(solution)/shard_map/cross_spectra/pallas_call | solution.py:438
  98.1 5.6 %finish.1 = bf16[2,32,320,320]{3,2,1,0:T(8,128)(2,1)} custom-call(bf16[2,27,320,320]{3,2,1,0:T(8,128)(2,1)S(1)} %get-tuple-element.7.begun, bf16[14,5,2,2,4,80,128]{6,5,4,3,2,1,0:T(8,128)(2,1)S(1)} %get-tuple-element.8.buf), custom_call_target="tpu_custom_call" | custom-call | tf_op jit(solution)/shard_map/finish/pallas_call | solution.py:460

commit v9 on v8

--- a/solution.py
+++ b/solution.py
@@ -35,7 +35,7 @@
     ("B", "products", 6),
     ("T", "relay_1", 2),
     ("T", "loop_1", 3),
-    ("B", "turn", -2),
+    ("B", "turn", -3),
     ("T", "loop_4", 2),
     ("S", "near_s", 2),
     ("T", "twin_a_t", 1),

time: 104 us -> 104 us (level)
  no operation moved by 1% of the time
where the time goes in v9:
time: 104 us
  Pallas kernels  104 us (100%)
    pallas_call x1, Pallas kernels, shards(): pl.pallas_call(kernel, out_shape=[jax.ShapeDtypeStruct((2, BEGUN, 320, 32...  98.1 us
    pallas_call x1, Pallas kernels, shards(): pl.pallas_call(finish_kernel, out_shape=jax.ShapeDtypeStruct((2, 32, 320,...  5.6 us

profile of v9, /device:TPU:10, one launch (start us, length us, event | category | flops | bytes accessed | tf_op | source)
XLA Modules:
  0.0 103.7 jit_solution(15263366079719877772)
XLA Ops:
  0.0 98.1 %cross_spectra.1 = (bf16[2,27,320,320]{3,2,1,0:T(8,128)(2,1)S(1)}, bf16[14,5,2,2,4,80,128]{6,5,4,3,2,1,0:T(8,128)(2,1)S(1)}) custom-call(bf16[512,512]{1,0:T(8,128)(2,1)} %constant.2.clone.dft_hbm, bf16[28,80,512]{2,1,0:T(8,128)(2,1)} %bitcast.2, s32[28,80]{1,0:T(8,128)} %bitcast.3), custom_call_target="tpu_custom_call" | custom-call | flops 12000000000 | bytes 20000000 | tf_op jit(solution)/shard_map/cross_spectra/pallas_call | solution.py:438
  98.1 5.6 %finish.1 = bf16[2,32,320,320]{3,2,1,0:T(8,128)(2,1)} custom-call(bf16[2,27,320,320]{3,2,1,0:T(8,128)(2,1)S(1)} %get-tuple-element.7.begun, bf16[14,5,2,2,4,80,128]{6,5,4,3,2,1,0:T(8,128)(2,1)S(1)} %get-tuple-element.8.buf), custom_call_target="tpu_custom_call" | custom-call | tf_op jit(solution)/shard_map/finish/pallas_call | solution.py:460
